TPU v7x, 256 devices: a whole 4x4x8 slice. The times are simulated.
256 devices in a mesh: dp: 16 (over z, y_lo), row: 4 (over x), col: 4 (over y_hi, core).
Axes of the slice: x: 4, y: 4 (y_hi: 2, y_lo: 2; y = y_hi * 2 + y_lo), z: 8, core: 2. Of those that a mesh axis runs over, the one named last changes fastest.
Arguments:
- inputs: bfloat16 [16, 96, 7680], P('dp', 'row', 'col'), may hold values from -6 to 6
- levels: bfloat16 [7680, 32768], P('row', ('dp', 'col')), may hold values from -4 to 4
- block_scales: float32 [60, 256], P('row', ('dp', 'col')), may hold values from 0.005705443 to 0.045643546
- grad_hidden: bfloat16 [16, 96, 32768], P(None, 'row', ('dp', 'col')), may hold values from -6 to 6
Outputs:
- hidden: bfloat16 [16, 96, 32768], P(None, 'row', ('dp', 'col'))
- grad_inputs: bfloat16 [16, 96, 7680], P('dp', 'row', 'col')
- grad_weight: bfloat16 [7680, 32768], P('row', ('dp', 'col'))
All inputs are finite; a program needn't handle non-finite values.
Results may differ from a plain program's by a relative error of at most 0.02.
Values may be sent and summed in bfloat16 or wider, within the bound.
A program may use at most 128 MiB of HBM per device.

v0:
```python
import jax
import jax.numpy as jnp
from jax import lax
from jax.sharding import PartitionSpec as P

inv_root_two = 0.7071067811865476
inv_root_two_pi = 0.3989422804014327


def gelu_pair(pre):
    normal_cdf = 0.5 * (1.0 + jax.scipy.special.erf(pre * inv_root_two))
    density = jnp.exp(-0.5 * pre * pre) * inv_root_two_pi
    return (pre * normal_cdf, normal_cdf + pre * density)


def shards(inputs, levels, block_scales, grad_hidden):
    nrow_blocks, ncol_blocks = block_scales.shape
    side = levels.shape[0] // nrow_blocks
    scaled = levels.reshape(nrow_blocks, side, ncol_blocks, side) * block_scales[:, None, :, None]
    weight = scaled.reshape(levels.shape).astype(jnp.bfloat16)
    wide_rows = lax.all_gather(inputs, "col", axis=2, tiled=True)
    gathered = lax.all_gather(wide_rows, "dp", axis=0, tiled=True)
    replica_count, block_tokens, full_width = gathered.shape
    tok_rows = gathered.reshape(replica_count * block_tokens, full_width)
    weight_cols = lax.all_gather(weight, "row", axis=0, tiled=True)
    pre = jnp.dot(tok_rows, weight_cols, preferred_element_type=jnp.float32)
    activated, slope = gelu_pair(pre)
    hidden = activated.astype(jnp.bfloat16).reshape(grad_hidden.shape)
    grad_pre = (
        grad_hidden.reshape(replica_count * block_tokens, -1).astype(jnp.float32) * slope
    ).astype(jnp.bfloat16)
    product = lax.dot_general(
        grad_pre, weight_cols, (((1,), (1,)), ((), ())), preferred_element_type=jnp.float32
    )
    col_count = lax.axis_size("col")
    quarter = full_width // col_count
    split_product = product.reshape(replica_count, block_tokens, col_count, quarter)
    grad_terms = split_product.transpose(0, 2, 1, 3).reshape(-1, quarter)
    own_grads = lax.psum_scatter(grad_terms, ("dp", "col"), scatter_dimension=0, tiled=True)
    grad_inputs = own_grads.reshape(1, block_tokens, quarter).astype(jnp.bfloat16)
    grad_weight = lax.psum_scatter(
        lax.dot_general(
            tok_rows, grad_pre, (((0,), (0,)), ((), ())), preferred_element_type=jnp.float32
        ).astype(jnp.bfloat16),
        "row",
        scatter_dimension=0,
        tiled=True,
    )
    return (hidden, grad_inputs, grad_weight)


def solution(mesh):
    placed = (
        P("dp", "row", "col"),
        P("row", ("dp", "col")),
        P("row", ("dp", "col")),
        P(None, "row", ("dp", "col")),
    )
    return jax.shard_map(
        shards,
        mesh=mesh,
        in_specs=placed,
        out_specs=(P(None, "row", ("dp", "col")), P("dp", "row", "col"), P("row", ("dp", "col"))),
        check_vma=False,
    )
```

profile of v0, /device:TPU:17, one launch (start us, length us, event | category | flops | bytes accessed | tf_op | source)
XLA Modules:
  0.0 648.9 jit_solution(13505120745376060348)
XLA Ops:
  7.2 0.0 copy-start.1
  7.2 0.0 all-gather.5.cloned.1.call-start
  7.2 9.0 %all_gather.10 = bf16[1,24,7680]{2,1,0:T(8,128)(2,1)} all-gather(bf16[1,24,1920]{2,1,0:T(8,128)(2,1)} %param.4), channel_id=1, replica_groups=mesh['dp'=16,'row'=4,'col'=4] {'col'}, dimensions={2}, use_global_device_ids=true | all-gather | bytes 460800 | tf_op jit(solution)/shard_map/all_gather | solution.py:21
  16.2 0.0 all-gather.5.cloned.1.call-update
  16.2 0.0 all-gather.3.cloned.1.call-start
  16.3 0.8 copy.10
  17.0 0.6 mul.47
  17.6 0.0 copy-start.2
  17.6 0.0 copy-done.1
  17.6 2.1 fusion.1
  19.7 0.0 all-gather.3.cloned.1.call-update
  19.8 0.0 reduce-scatter.10.cloned.1.call-start
  19.8 131.3 %all-gather.5.cloned.1.call-done = bf16[16,24,7680]{2,1,0:T(8,128)(2,1)} async-done(((bf16[1,24,7680]{2,1,0:T(8,128)(2,1)}), bf16[16,24,7680]{2,1,0:T(8,128)(2,1)}) %all-gather.5.cloned.1.call-update) | async-done | bytes 5898256 | tf_op jit(solution)/shard_map/all_gather | solution.py:22
  151.1 85.5 %all-gather.3.cloned.1.call-done = bf16[7680,512]{1,0:T(8,128)(2,1)} async-done(((bf16[1920,512]{1,0:T(8,128)(2,1)}), bf16[7680,512]{1,0:T(8,128)(2,1)}) %all-gather.3.cloned.1.call-update) | async-done | bytes 7864336 | tf_op jit(solution)/shard_map/all_gather | solution.py:25
  236.6 0.0 copy-done.2
  236.6 0.0 copy-start
  236.6 9.3 %fusion.7 = (bf16[384,512]{1,0:T(8,128)(2,1)S(1)}, bf16[384,512]{1,0:T(8,128)(2,1)}) fusion(bf16[16,24,512]{2,1,0:T(8,128)(2,1)S(1)} %copy-done.2, bf16[384,7680]{1,0:T(8,128)(2,1)} %bitcast.30, bf16[7680,512]{1,0:T(8,128)(2,1)} %all-gather.3.cloned.1.call-done), kind=kOutput, calls=%fused_computation.11 | convolution fusion | flops 3022454784 | bytes 14942208 | tf_op jit(solution)/shard_map/dot_general | solution.py:26
  245.9 0.0 copy-done
  245.9 6.1 fusion.8
  252.0 14.1 %reshape.29 = f32[16,24,4,1920]{3,2,1,0:T(4,128)} reshape(f32[384,7680]{1,0:T(8,128)} %fusion.8) | data formatting | bytes 23592960 | tf_op jit(solution)/shard_map/reshape | solution.py:37
  266.1 9.5 %copy.11 = f32[16,4,24,1920]{3,2,1,0:T(8,128)} copy(f32[16,4,24,1920]{3,1,2,0:T(4,128)} %bitcast.28) | data formatting | bytes 23592960 | tf_op jit(solution)/shard_map/transpose | solution.py:38
  275.6 0.0 reduce-scatter.10.cloned.1.call-update
  275.6 0.0 reduce-scatter.8.cloned.1.call-start
  275.6 9.2 %fusion = bf16[7680,512]{0,1:T(8,128)(2,1)} fusion(bf16[384,512]{1,0:T(8,128)(2,1)S(1)} %get-tuple-element.9, bf16[384,7680]{1,0:T(8,128)(2,1)} %bitcast.31), kind=kOutput, calls=%fused_computation.1 | convolution fusion | flops 3023831040 | bytes 14155776 | tf_op jit(solution)/shard_map/dot_general | solution.py:42
  284.8 10.7 %copy.13 = bf16[7680,512]{1,0:T(8,128)(2,1)} copy(bf16[7680,512]{0,1:T(8,128)(2,1)} %fusion) | data formatting | bytes 15728640
  295.5 0.0 reduce-scatter.8.cloned.1.call-update
  295.5 260.7 %reduce-scatter.10.cloned.1.call-done = f32[24,1920]{1,0:T(8,128)} async-done(((f32[1536,1920]{1,0:T(8,128)}), f32[24,1920]{1,0:T(8,128)}) %reduce-scatter.10.cloned.1.call-update) | async-done | bytes 184336
  556.2 1.6 convert_bitcast_fusion
  557.8 84.6 %reduce-scatter.8.cloned.1.call-done = bf16[1920,512]{1,0:T(8,128)(2,1)} async-done(((bf16[7680,512]{1,0:T(8,128)(2,1)}), bf16[1920,512]{1,0:T(8,128)(2,1)}) %reduce-scatter.8.cloned.1.call-update) | async-done | bytes 1966096
Async XLA Ops:
  7.2 10.5 %copy-start.1 = (bf16[1920,512]{1,0:T(8,128)(2,1)S(1)}, bf16[1920,512]{1,0:T(8,128)(2,1)}, u32[]{:S(2)}) copy-start(bf16[1920,512]{1,0:T(8,128)(2,1)} %param.5) | copy-start | bytes 5898244
  7.2 143.9 %all-gather.5.cloned.1.call-start = ((), (), s32[]{:S(2)}) async-start(), calls=%async_computation.3 | async-start | bytes 6266880 | tf_op jit(solution)/shard_map/all_gather | solution.py:22
  16.2 220.4 %all-gather.3.cloned.1.call-start = ((), (), s32[]{:S(2)}) async-start(), calls=%async_computation.2 | async-start | bytes 9830400 | tf_op jit(solution)/shard_map/all_gather | solution.py:25
  17.6 219.0 %copy-start.2 = (bf16[16,24,512]{2,1,0:T(8,128)(2,1)S(1)}, bf16[16,24,512]{2,1,0:T(8,128)(2,1)}, u32[]{:S(2)}) copy-start(bf16[16,24,512]{2,1,0:T(8,128)(2,1)} %param.7) | copy-start | bytes 1179652
  19.8 536.5 %reduce-scatter.10.cloned.1.call-start = ((), (), s32[]{:S(2)}) async-start(), calls=%async_computation.5 | async-start | bytes 11980800
  236.6 9.3 %copy-start = (bf16[7680,512]{1,0:T(8,128)(2,1)S(1)}, bf16[7680,512]{1,0:T(8,128)(2,1)}, u32[]{:S(2)}) copy-start(bf16[7680,512]{1,0:T(8,128)(2,1)} %all-gather.3.cloned.1.call-done) | copy-start | bytes 23592964
  275.6 366.8 %reduce-scatter.8.cloned.1.call-start = ((), (), s32[]{:S(2)}) async-start(), calls=%async_computation.4 | async-start | bytes 9830400
Sparse Core Ops, SparseCore 0:
  16.3 134.7 all-gather.4
  153.5 83.0 all-gather.2
  275.7 280.4 reduce-scatter.9
  559.2 83.1 reduce-scatter.7
where the time goes:
time: 651 us; the launch traced here: 649 us
  waiting for transfers between devices  562 us (86%)
  local copies, waits for them, and re-layouts  35.6 us (5%)
  matrix products  24.6 us (4%)
  between operations  13.8 us (2%)
  blocking collectives  8.98 us (1%)
    unnamed x6, waiting for transfers between devices  345 us
    all_gather x1, waiting for transfers between devices, shards(): gathered = lax.all_gather(wide_rows, 'dp', axis=0, tiled=True)  131 us
    all_gather x1, waiting for transfers between devices, shards(): weight_cols = lax.all_gather(weight, 'row', axis=0, tiled=True)  85.5 us
    reshape x1, local copies, waits for them, and re-layouts, shards(): product.reshape(replica_count, block_tokens, col_count, quarter)  14.1 us
  transfers between devices with their start and end apart: 4, of which 4 were waited for; matrix products, arithmetic and copies ran while one was open for 4% of the time, Pallas kernels for 0%

commit v1 on v0

v1 whole, which is shorter than its diff:
```python
import jax
import jax.numpy as jnp
from jax import lax
from jax.sharding import PartitionSpec as P

inv_root_two = 0.7071067811865476
inv_root_two_pi = 0.3989422804014327


def gelu_pair(pre):
    normal_cdf = 0.5 * (1.0 + jax.scipy.special.erf(pre * inv_root_two))
    density = jnp.exp(-0.5 * pre * pre) * inv_root_two_pi
    return (pre * normal_cdf, normal_cdf + pre * density)


def swap_row_col(x, n):
    return lax.ppermute(x, ("row", "col"), [(r * n + c, c * n + r) for r in range(n) for c in range(n)])


def shards(inputs, levels, block_scales, grad_hidden):
    nrow_blocks, ncol_blocks = block_scales.shape
    side = levels.shape[0] // nrow_blocks
    scaled = levels.reshape(nrow_blocks, side, ncol_blocks, side) * block_scales[:, None, :, None]
    weight = scaled.reshape(levels.shape).astype(jnp.bfloat16)
    n = lax.axis_size("row")
    block_tokens, feats = inputs.shape[1:]
    replicas = grad_hidden.shape[0]
    mine = swap_row_col(inputs[0], n)
    tok_rows = lax.all_gather(mine, ("dp", "col"), axis=0, tiled=False).reshape(replicas, n, block_tokens, feats)
    tok_rows = tok_rows.transpose(1, 0, 2, 3).reshape(n * replicas * block_tokens, feats)
    part = jnp.dot(tok_rows, weight, preferred_element_type=jnp.float32).astype(jnp.bfloat16)
    pre = lax.psum_scatter(part, "row", scatter_dimension=0, tiled=True).astype(jnp.float32)
    activated, slope = gelu_pair(pre)
    hidden = activated.astype(jnp.bfloat16).reshape(grad_hidden.shape)
    grad_pre = (grad_hidden.reshape(pre.shape).astype(jnp.float32) * slope).astype(jnp.bfloat16)
    all_grad = lax.all_gather(grad_pre, "row", axis=0, tiled=True)
    product = lax.dot_general(
        all_grad, weight, (((1,), (1,)), ((), ())), preferred_element_type=jnp.float32
    ).astype(jnp.bfloat16)
    terms = product.reshape(n, replicas, block_tokens, feats).transpose(1, 0, 2, 3).reshape(-1, feats)
    own = lax.psum_scatter(terms, ("dp", "col"), scatter_dimension=0, tiled=True)
    grad_inputs = swap_row_col(own.astype(jnp.bfloat16), n)[None]
    grad_weight = lax.dot_general(
        tok_rows, all_grad, (((0,), (0,)), ((), ())), preferred_element_type=jnp.float32
    ).astype(jnp.bfloat16)
    return (hidden, grad_inputs, grad_weight)


def solution(mesh):
    placed = (
        P("dp", "row", "col"),
        P("row", ("dp", "col")),
        P("row", ("dp", "col")),
        P(None, "row", ("dp", "col")),
    )
    return jax.shard_map(
        shards,
        mesh=mesh,
        in_specs=placed,
        out_specs=(P(None, "row", ("dp", "col")), P("dp", "row", "col"), P("row", ("dp", "col"))),
        check_vma=False,
    )
```

time: 651 us -> 514 us (0.79)
  waiting for transfers between devices: 562 us -> 445 us
  starting transfers between devices: 0.16 us -> 20.6 us
  local copies, waits for them, and re-layouts: 35.6 us -> 15.9 us
  blocking collectives: 8.98 us -> 0 us
  matrix products: 24.6 us -> 16.8 us
    unnamed x6 -> x5, waiting for transfers between devices: 345 us -> 265 us
    all_gather x2, waiting for transfers between devices: 217 us -> 148 us  [the longest x1 118 us: shards(): lax.all_gather(mine, ('dp', 'col'), axis=0, tiled=False)]
    reduce_scatter x0 -> x1, waiting for transfers between devices: none -> 26.3 us  [shards(): lax.psum_scatter(part, 'row', scatter_dimension=0, tiled=True)]
    ppermute x0 -> x2, starting transfers between devices: none -> 20.5 us  [swap_row_col(): lax.ppermute(x, ('row', 'col'), [(r * n + c, c * n + r) for r in range(n)...]
    reshape x1 -> x0, local copies, waits for them, and re-layouts: 14.1 us -> none  [shards(): product.reshape(replica_count, block_tokens, col_count, quarter)]
    all_gather x1 -> x0, blocking collectives: 8.98 us -> none  [shards(): wide_rows = lax.all_gather(inputs, 'col', axis=2, tiled=True)]
    dot_general x3, matrix products: 24.6 us -> 16.8 us  [the longest x1 6.67 us: shards(): lax.dot_general(all_grad, weight, (((1,), (1,)), ((), ())), preferred_ele...]
  transfers between devices with their start and end apart: 4 -> 6, of which waited for: 4 -> 5; matrix products, arithmetic and copies ran while one was open for 4% -> 2% of each run, Pallas kernels for 0% -> 0%
where the time goes in v1:
time: 514 us
  waiting for transfers between devices  445 us (87%)
  starting transfers between devices  20.6 us (4%)
  matrix products  16.8 us (3%)
  local copies, waits for them, and re-layouts  15.9 us (3%)
  between operations  13.9 us (3%)
    unnamed x5, waiting for transfers between devices  265 us
    all_gather x1, waiting for transfers between devices, shards(): lax.all_gather(mine, ('dp', 'col'), axis=0, tiled=False)  118 us
    all_gather x1, waiting for transfers between devices, shards(): all_grad = lax.all_gather(grad_pre, 'row', axis=0, tiled=True)  29.9 us
    reduce_scatter x1, waiting for transfers between devices, shards(): lax.psum_scatter(part, 'row', scatter_dimension=0, tiled=True)  26.3 us
    ppermute x2, starting transfers between devices, swap_row_col(): lax.ppermute(x, ('row', 'col'), [(r * n + c, c * n + r) for r in range(n)...  20.5 us
  transfers between devices with their start and end apart: 6, of which 5 were waited for; matrix products, arithmetic and copies ran while one was open for 2% of the time, Pallas kernels for 0%

profile of v1, /device:TPU:17, one launch (start us, length us, event | category | flops | bytes accessed | tf_op | source)
XLA Modules:
  0.0 514.1 jit_solution(16051537952848155013)
XLA Ops:
  7.2 0.0 all-gather.6.cloned.1.call-start
  7.2 4.7 collective-permute-start
  11.9 6.2 %collective-permute-done = bf16[24,1920]{1,0:T(8,128)(2,1)S(1)} collective-permute-done((bf16[24,1920]{1,0:T(8,128)(2,1)}, bf16[24,1920]{1,0:T(8,128)(2,1)S(1)}, u32[]{:S(2)}, u32[]{:S(2)}) %collective-permute-start) | collective-permute-done | bytes 92192 | tf_op jit(solution)/shard_map/ppermute | solution.py:17
  18.1 0.0 copy-start.3
  18.1 0.6 copy-done.3
  18.7 0.0 all-gather.6.cloned.1.call-update
  18.8 0.0 reduce-scatter.8.cloned.1.call-start
  18.8 0.8 copy.23
  19.6 117.7 %all-gather.6.cloned.1.call-done = bf16[1536,1920]{1,0:T(8,128)(2,1)} async-done(((bf16[24,1920]{1,0:T(8,128)(2,1)}), bf16[1536,1920]{1,0:T(8,128)(2,1)}) %all-gather.6.cloned.1.call-update) | async-done | bytes 5898256 | tf_op jit(solution)/shard_map/all_gather | solution.py:29
  137.3 3.1 copy.24
  140.4 0.0 copy-start
  140.4 0.0 copy-start.4
  140.4 0.6 mul.47
  141.0 0.0 copy-start.1
  141.0 2.1 copy-done
  143.1 1.2 copy-done.1
  144.3 0.0 copy-done.4
  144.3 3.5 fusion.1
  147.8 0.0 copy-start.2
  147.8 1.6 copy.28
  149.4 0.0 reduce-scatter.8.cloned.1.call-update
  149.4 0.0 all-gather.4.cloned.1.call-start
  149.5 26.3 %reduce-scatter.8.cloned.1.call-done = bf16[384,512]{1,0:T(8,128)(2,1)} async-done(((bf16[1536,512]{1,0:T(8,128)(2,1)}), bf16[384,512]{1,0:T(8,128)(2,1)}) %reduce-scatter.8.cloned.1.call-update) | async-done | bytes 393232 | tf_op jit(solution)/shard_map/reduce_scatter | solution.py:32
  175.8 0.0 copy-done.2
  175.8 2.3 fusion.11
  178.0 0.0 all-gather.4.cloned.1.call-update
  178.1 0.0 reduce-scatter.10.cloned.1.call-start
  178.1 29.9 %all-gather.4.cloned.1.call-done = bf16[1536,512]{1,0:T(8,128)(2,1)} async-done(((bf16[384,512]{1,0:T(8,128)(2,1)}), bf16[1536,512]{1,0:T(8,128)(2,1)}) %all-gather.4.cloned.1.call-update) | async-done | bytes 1572880 | tf_op jit(solution)/shard_map/all_gather | solution.py:36
  208.1 6.7 %convolution_convert_fusion = bf16[1536,1920]{1,0:T(8,128)(2,1)S(1)} fusion(bf16[1536,512]{1,0:T(8,128)(2,1)} %all-gather.4.cloned.1.call-done, f32[240,8,4,128]{3,2,1,0:T(4,128)} %bitcast.38, bf16[1920,512]{1,0:T(8,128)(2,1)} %param.5), kind=kOutput, calls=%fused_computation | convolution fusion | flops 3025797120 | bytes 13369344 | tf_op jit(solution)/shard_map/dot_general | solution.py:37
  214.7 3.0 copy.26
  217.7 0.0 reduce-scatter.10.cloned.1.call-update
  217.8 264.5 %reduce-scatter.10.cloned.1.call-done = bf16[24,1920]{1,0:T(8,128)(2,1)} async-done(((bf16[1536,1920]{1,0:T(8,128)(2,1)}), bf16[24,1920]{1,0:T(8,128)(2,1)}) %reduce-scatter.10.cloned.1.call-update) | async-done | bytes 92176
  482.3 15.7 %collective-permute-start.1 = (bf16[24,1920]{1,0:T(8,128)(2,1)}, bf16[24,1920]{1,0:T(8,128)(2,1)S(1)}, u32[]{:S(2)}, u32[]{:S(2)}) collective-permute-start(bf16[24,1920]{1,0:T(8,128)(2,1)} %reduce-scatter.10.cloned.1.call-done), channel_id=1, source_target_pairs={{0,0},{1,4},{2,8},{3,12},{4,1},{5,5},{6,9},{7,13},{8,2},{9,6},{10,... | collective-permute-start | bytes 276488 | tf_op jit(solution)/shard_map/ppermute | solution.py:17
  498.0 6.6 %fusion.2 = bf16[1920,512]{0,1:T(8,128)(2,1)S(1)} fusion(bf16[1536,512]{1,0:T(8,128)(2,1)} %all-gather.4.cloned.1.call-done, bf16[1536,1920]{1,0:T(8,128)(2,1)} %bitcast.34), kind=kOutput, calls=%fused_computation.6 | convolution fusion | flops 3020881920 | bytes 9437184 | tf_op jit(solution)/shard_map/dot_general | solution.py:43
  504.7 2.3 copy.27
  507.0 0.0 collective-permute-done.1
  507.0 0.6 copy.35
Async XLA Ops:
  7.2 130.1 %all-gather.6.cloned.1.call-start = ((), (), s32[]{:S(2)}) async-start(), calls=%async_computation.3 | async-start | bytes 5990400 | tf_op jit(solution)/shard_map/all_gather | solution.py:29
  7.2 10.9 %collective-permute-start = (bf16[24,1920]{1,0:T(8,128)(2,1)}, bf16[24,1920]{1,0:T(8,128)(2,1)S(1)}, u32[]{:S(2)}, u32[]{:S(2)}) collective-permute-start(bf16[24,1920]{1,0:T(8,128)(2,1)} %bitcast.41), channel_id=1, source_target_pairs={{0,0},{1,4},{2,8},{3,12},{4,1},{5,5},{6,9},{7,13},{8,2},{9,6},{10,... | collective-permute-start | bytes 276488 | tf_op jit(solution)/shard_map/ppermute | solution.py:17
  18.1 0.6 copy-start.3
  18.8 157.0 %reduce-scatter.8.cloned.1.call-start = ((), (), s32[]{:S(2)}) async-start(), calls=%async_computation.4 | async-start | bytes 1966080 | tf_op jit(solution)/shard_map/reduce_scatter | solution.py:32
  140.4 2.7 copy-start
  140.4 3.9 copy-start.4
  141.0 3.3 copy-start.1
  147.8 28.0 %copy-start.2 = (bf16[16,24,512]{2,1,0:T(8,128)(2,1)S(1)}, bf16[16,24,512]{2,1,0:T(8,128)(2,1)}, u32[]{:S(2)}) copy-start(bf16[16,24,512]{2,1,0:T(8,128)(2,1)} %param.7) | copy-start | bytes 1179652
  149.4 58.6 %all-gather.4.cloned.1.call-start = ((), (), s32[]{:S(2)}) async-start(), calls=%async_computation.2 | async-start | bytes 1966080 | tf_op jit(solution)/shard_map/all_gather | solution.py:36
  178.1 304.2 %reduce-scatter.10.cloned.1.call-start = ((), (), s32[]{:S(2)}) async-start(), calls=%async_computation.5 | async-start | bytes 5990400
  482.3 24.7 %collective-permute-start.1 = (bf16[24,1920]{1,0:T(8,128)(2,1)}, bf16[24,1920]{1,0:T(8,128)(2,1)S(1)}, u32[]{:S(2)}, u32[]{:S(2)}) collective-permute-start(bf16[24,1920]{1,0:T(8,128)(2,1)} %reduce-scatter.10.cloned.1.call-done), channel_id=1, source_target_pairs={{0,0},{1,4},{2,8},{3,12},{4,1},{5,5},{6,9},{7,13},{8,2},{9,6},{10,... | collective-permute-start | bytes 276488 | tf_op jit(solution)/shard_map/ppermute | solution.py:17
Sparse Core Ops, SparseCore 0:
  18.9 118.3 all-gather.5
  149.5 26.1 reduce-scatter.7
  178.2 29.8 all-gather.3
  217.9 264.3 reduce-scatter.9

commit v2 on v1

v2 whole, which is shorter than its diff:
```python
import functools

import jax
import jax.numpy as jnp
from jax import lax
from jax.experimental import pallas as pl
from jax.experimental.pallas import tpu as pltpu
from jax.sharding import PartitionSpec as P

inv_root_two = 0.7071067811865476
inv_root_two_pi = 0.3989422804014327
bf16, f32 = jnp.bfloat16, jnp.float32

NZ, NY, NX = 8, 4, 4
ROWS = 48
U = 16
D4 = 1920
H = 512
BW = 1024
BO = 896
GROUPS = ((0, 3), (3, 5), (5, 8))
N_SEND, N_RECV = 144, 144


def pos_f(k):
    return 0 if k == 0 else 2 * k - 1


def pos_b(k):
    return 2 * k


def sib_pos(p):
    if p == 0 or p == 7:
        return p
    return p + 1 if p % 2 else p - 1


def gelu_pair(pre):
    normal_cdf = 0.5 * (1.0 + lax.erf(pre * inv_root_two))
    density = jnp.exp(-0.5 * pre * pre) * inv_root_two_pi
    return (pre * normal_cdf, normal_cdf + pre * density)


def kernel(inp, lev, scl, gh, hid, gin, gw,
           W, S0, R0, X, PS, PR, GP, GI, CA, CB,
           A1s, Ass, A2s, A1r, Asr, A2r, YA,
           ZLs, ZLr, ZSs, ZSr, BLs, BLr, BSs, BSr, YB,
           Y1s, Yss, Y2s, Y1r, Ysr, Y2r, FA, FB, OA, OB,
           ssem, rsem):
    dp, x, col = lax.axis_index("dp"), lax.axis_index("row"), lax.axis_index("col")
    z, ylo, yhi, core = dp // 2, dp % 2, col // 2, col % 2
    y = 2 * yhi + ylo
    s = 1 - 2 * core

    def dev(zz, yy, xx, cc):
        return {"dp": zz * 2 + yy % 2, "row": xx, "col": (yy // 2) * 2 + cc}

    sources = [dev(z, 2 * (x // 2) + j, y, x % 2) for j in range(2)]
    targets = [dev(z, x, 2 * yhi + core, c) for c in range(2)]
    loops = (x == y) & (core == x % 2)
    z_f, z_b = dev((z + s + NZ) % NZ, y, x, core), dev((z - s + NZ) % NZ, y, x, core)
    y_f, y_b = dev(z, (y + s + NY) % NY, x, core), dev(z, (y - s + NY) % NY, x, core)
    sib = dev(z, y, x, 1 - core)
    yf1, yb1, yf2 = (y - s + NY) % NY, (y + s + NY) % NY, (y + 2) % NY
    x_dev = [None] + [dev(z, y, (x + d) % NX, core) for d in range(1, NX)]

    sends, keys, sent = [], {}, [0]

    def rid(key):
        if key not in keys:
            keys[key] = len(keys)
        return rsem.at[keys[key]]

    def copy(src, dst, key, to):
        i = sent[0]
        sent[0] += 1
        return pltpu.make_async_remote_copy(src, dst, ssem.at[i], rid(key), device_id=to)

    def send(src, dst, key, to):
        c = copy(src, dst, key, to)
        c.start()
        sends.append(c)

    def arrived(dst, key):
        pltpu.make_async_remote_copy(dst, dst, ssem.at[0], rid(key), device_id=sib).wait_recv()

    bar = pltpu.get_barrier_semaphore()
    partners = sources + targets + x_dev[1:] + [z_f, z_b, y_f, y_b, sib]
    for d in partners:
        pl.semaphore_signal(bar, 1, device_id=d)
    S0[...] = jnp.concatenate([inp[...].astype(f32), jnp.zeros((8, D4), f32)], 0).astype(bf16)
    pl.semaphore_wait(bar, len(partners))

    slot = ylo
    swaps = []
    for c in range(2):
        i = sent[0]
        sent[0] += 1
        swaps.append(pltpu.make_async_remote_copy(S0, R0.at[slot], ssem.at[i], rsem.at[slot], device_id=targets[c]))
    for j in range(2):
        rid(("swap", j))
    for c in range(2):
        mine = loops & (core == c)

        @pl.when(jnp.logical_not(mine))
        def _():
            swaps[c].start()

        @pl.when(mine)
        def _():
            R0[slot] = S0[...]

    @pl.loop(0, D4 // 128)
    def _(a):
        r = pl.ds(pl.multiple_of(a * 128, 128), 128)
        for b in range(H // 128):
            cs = pl.ds(b * 128, 128)
            W[r, cs] = (lev[r, cs].astype(f32) * scl[a, b]).astype(bf16)

    for j in range(2):

        @pl.when(jnp.logical_not(loops & (j == x % 2)))
        def _():
            arrived(R0.at[j], ("swap", j))

    X[y, 0] = jnp.concatenate([R0[0].astype(f32)[:24], R0[1].astype(f32)[:24]], 0).astype(bf16)

    r_mine = pl.ds(pl.multiple_of(core * U, U), U)
    r_other = pl.ds(pl.multiple_of((1 - core) * U, U), U)
    r_b = pl.ds(2 * U, U)
    c_mine = pl.ds(pl.multiple_of(core * BO, 128), BW)
    c_other = pl.ds(pl.multiple_of((1 - core) * BO, 128), BW)
    c_give = pl.ds(pl.multiple_of(core * BW, 128), BO)
    c_take = pl.ds(pl.multiple_of((1 - core) * BW, 128), BO)

    def a_unit(yq, p):
        return X.at[yq, p, r_mine]

    def b_unit(yq, p):
        return X.at[yq, p, r_b, c_mine]

    def b_group(p):
        return X.at[:, p, r_b, c_mine]

    def at_dist(k):
        return [0] if k == 0 else [pos_f(k)] + ([pos_b(k)] if k < 4 else [])

    def y_start(p):
        send(a_unit(y, p), a_unit(y, p), ("Ay", p, 1), y_f)
        send(a_unit(y, p), a_unit(y, p), ("Ay", p, -1), y_b)

    def y_hop1(p):
        arrived(a_unit(yf1, p), ("Ay", p, 1))
        send(a_unit(yf1, p), a_unit(yf1, p), ("Ay", p, 2), y_f)
        if p == 0:
            send(a_unit(yf1, 0), a_unit(yf1, 0), ("As0", -1), sib)
        arrived(a_unit(yb1, p), ("Ay", p, -1))
        if p == 0:
            send(a_unit(yb1, 0), a_unit(yb1, 0), ("As0", 1), sib)

    def y_hop2(p):
        arrived(a_unit(yf2, p), ("Ay", p, 2))
        if p == 0:
            send(a_unit(yf2, 0), a_unit(yf2, 0), ("As0", 2), sib)
        else:
            send(X.at[:, p, r_mine], X.at[:, sib_pos(p), r_mine], ("As", sib_pos(p)), sib)

    def bz_send(k):
        if k < 4:
            send(b_group(pos_f(k)), b_group(pos_f(k + 1)), ("Bz", pos_f(k + 1)), z_f)
        if k < 3:
            send(b_group(pos_b(k)), b_group(pos_b(k + 1)), ("Bz", pos_b(k + 1)), z_b)

    def bz_hop(k):
        for p in at_dist(k):
            arrived(b_group(p), ("Bz", p))
        bz_send(k)
        for p in at_dist(k):
            send(X.at[:, p, r_b, c_give], X.at[:, sib_pos(p), r_b, c_give], ("Bs", sib_pos(p)), sib)

    def sib_wait(k):
        for p in at_dist(k):
            if p == 0:
                for q, yq in ((1, yf1), (-1, yb1), (2, yf2)):
                    arrived(X.at[yq, 0, r_other], ("As0", q))
                    arrived(X.at[yq, 0, r_b, c_take], ("Bs0", q))
            else:
                arrived(X.at[:, p, r_other], ("As", p))
                arrived(X.at[:, p, r_b, c_take], ("Bs", p))

    def az_send(k):
        if k < 4:
            send(a_unit(y, pos_f(k)), a_unit(y, pos_f(k + 1)), ("Az", pos_f(k + 1)), z_f)
        if k < 3:
            send(a_unit(y, pos_b(k)), a_unit(y, pos_b(k + 1)), ("Az", pos_b(k + 1)), z_b)

    def tick(k):
        if k == 0:
            az_send(0)
            y_start(0)
            send(b_unit(y, 0), b_unit(y, 0), ("By", 1), y_f)
            send(b_unit(y, 0), b_unit(y, 0), ("By", -1), y_b)
            return
        if k <= 4:
            for p in at_dist(k):
                arrived(a_unit(y, p), ("Az", p))
            az_send(k)
            for p in at_dist(k):
                y_start(p)
        if k == 1:
            arrived(b_unit(yf1, 0), ("By", 1))
            send(b_unit(yf1, 0), b_unit(yf1, 0), ("By", 2), y_f)
            arrived(b_unit(yb1, 0), ("By", -1))
            send(X.at[yf1, 0, r_b, c_give], X.at[yf1, 0, r_b, c_give], ("Bs0", -1), sib)
            send(X.at[yb1, 0, r_b, c_give], X.at[yb1, 0, r_b, c_give], ("Bs0", 1), sib)
        if k == 2:
            arrived(b_unit(yf2, 0), ("By", 2))
            bz_send(0)
            send(X.at[yf2, 0, r_b, c_give], X.at[yf2, 0, r_b, c_give], ("Bs0", 2), sib)
        if k - 1 <= 4:
            for p in at_dist(k - 1):
                y_hop1(p)
        if 3 <= k <= 6:
            bz_hop(k - 2)
        if k >= 2:
            for p in at_dist(k - 2):
                y_hop2(p)

    def partial_pre(g):
        p0, p1 = GROUPS[g]
        m = (p1 - p0) * ROWS
        for h in range(0, H, 256):
            rows = X[:, p0:p1].reshape(NY * m, D4)
            part = jnp.dot(rows, W[:, h:h + 256], preferred_element_type=f32)
            PS[:, p0:p1, :, h:h + 256] = part.astype(bf16).reshape(NY, p1 - p0, ROWS, 256)
        for d in range(1, NX):
            t = (x + d) % NX
            send(PS.at[t, p0:p1], PR.at[d - 1, p0:p1], ("pre", g, d), x_dev[d])

    def activate(g):
        p0, p1 = GROUPS[g]
        for d in range(1, NX):
            arrived(PR.at[d - 1, p0:p1], ("pre", g, d))

        @pl.loop(p0, p1)
        def _(p):
            k = (p + 1) // 2
            zz = (z + (1 - 2 * (p % 2)) * k * s + NZ) % NZ
            pre = PS[x, p].astype(f32)
            for d in range(NX - 1):
                pre += PR[d, p].astype(f32)
            activated, slope = gelu_pair(pre)
            hid[zz] = activated.astype(bf16)
            GP[x, p] = (gh[zz].astype(f32) * slope).astype(bf16)

        for d in range(1, NX):
            send(GP.at[x, p0:p1], GP.at[x, p0:p1], ("gp", g, d), x_dev[d])

    def grad_wait(g):
        p0, p1 = GROUPS[g]
        for d in range(1, NX):
            arrived(GP.at[(x - d + NX) % NX, p0:p1], ("gp", g, d))

    def input_terms(g):
        p0, p1 = GROUPS[g]
        m = (p1 - p0) * ROWS
        grad_wait(g)

        @pl.loop(0, D4 // 384)
        def _(n):
            cs = pl.ds(pl.multiple_of(n * 384, 128), 384)
            rows = GP[:, p0:p1].reshape(NY * m, H)
            part = lax.dot_general(rows, W[cs, :], (((1,), (1,)), ((), ())), preferred_element_type=f32)
            GI[:, p0:p1, :, cs] = part.astype(bf16).reshape(NY, p1 - p0, ROWS, 384)

        for p in reversed(range(p0, p1)):
            q = sib_pos(p)
            send(GI.at[:, p, r_b, c_other], CB.at[:, q], ("CB", q), sib)
            send(GI.at[:, p, r_other], CA.at[:, q], ("CA", q), sib)

    def a_term(yq, p):
        return GI[yq, p, r_mine].astype(f32) + CA[yq, p].astype(f32)

    def ay_begin(g):
        p0, p1 = GROUPS[g]
        for p in range(p0, p1):
            arrived(CA.at[:, p], ("CA", p))

        @pl.loop(p0, p1)
        def _(p):
            A1s[p] = a_term(yf2, p).astype(bf16)
            Ass[p] = a_term(yb1, p).astype(bf16)

        send(A1s.at[p0:p1], A1r.at[p0:p1], ("A1", g), y_b)
        send(Ass.at[p0:p1], Asr.at[p0:p1], ("As_", g), y_f)

    def ay_middle(g):
        p0, p1 = GROUPS[g]
        arrived(A1r.at[p0:p1], ("A1", g))

        @pl.loop(p0, p1)
        def _(p):
            A2s[p] = (a_term(yf1, p) + A1r[p].astype(f32)).astype(bf16)

        send(A2s.at[p0:p1], A2r.at[p0:p1], ("A2", g), y_b)

    def ay_end(g):
        p0, p1 = GROUPS[g]
        arrived(Asr.at[p0:p1], ("As_", g))
        arrived(A2r.at[p0:p1], ("A2", g))

        @pl.loop(p0, p1)
        def _(p):
            YA[p] = a_term(y, p) + Asr[p].astype(f32) + A2r[p].astype(f32)

    def b_terms(p):
        return GI[:, p, r_b, c_mine].astype(f32) + CB[:, p].astype(f32)

    def z_chain(j, term, ls, lr, ss, sr, name):
        if j == 0:
            ls[0] = term(pos_f(4)).astype(bf16)
            ss[0] = term(pos_b(3)).astype(bf16)
        else:
            arrived(lr.at[j - 1], (name, "L", j))
            if j < 4:
                ls[j] = (term(pos_f(4 - j)) + lr[j - 1].astype(f32)).astype(bf16)
            if j < 4:
                arrived(sr.at[j - 1], (name, "S", j))
            if j < 3:
                ss[j] = (term(pos_b(3 - j)) + sr[j - 1].astype(f32)).astype(bf16)
        if j < 4:
            send(ls.at[j], lr.at[j], (name, "L", j + 1), z_b)
        if j < 3:
            send(ss.at[j], sr.at[j], (name, "S", j + 1), z_f)
        if j == 4:
            return term(0) + lr[3].astype(f32) + sr[2].astype(f32)

    def weight_grad(n0, n1):
        @pl.loop(n0, n1)
        def _(n):
            cs = pl.ds(pl.multiple_of(n * 128, 128), 128)
            rows = X[:, :, :, cs].reshape(NY * NZ * ROWS, 128)
            part = lax.dot_general(
                rows, GP[...].reshape(NY * NZ * ROWS, H), (((0,), (0,)), ((), ())), preferred_element_type=f32
            )
            gw[cs, :] = part.astype(bf16)

    for k in range(4):
        tick(k)
    sib_wait(0)
    sib_wait(1)
    partial_pre(0)
    tick(4)
    sib_wait(2)
    partial_pre(1)
    tick(5)
    activate(0)
    tick(6)
    sib_wait(3)
    sib_wait(4)
    partial_pre(2)
    activate(1)
    input_terms(0)
    input_terms(1)
    ay_begin(0)
    activate(2)
    ay_middle(0)
    ay_begin(1)
    ay_end(0)
    input_terms(2)
    ay_middle(1)
    for p in range(NZ):
        arrived(CB.at[:, p], ("CB", p))
    z_chain(0, b_terms, BLs, BLr, BSs, BSr, "B")
    ay_begin(2)
    ay_end(1)
    weight_grad(0, 4)
    z_chain(1, b_terms, BLs, BLr, BSs, BSr, "B")
    ay_middle(2)
    weight_grad(4, 8)
    z_chain(2, b_terms, BLs, BLr, BSs, BSr, "B")
    ay_end(2)
    a_final = functools.partial(z_chain, term=lambda p: YA[p], ls=ZLs, lr=ZLr, ss=ZSs, sr=ZSr, name="A")
    a_final(0)
    weight_grad(8, 11)
    z_chain(3, b_terms, BLs, BLr, BSs, BSr, "B")
    a_final(1)
    weight_grad(11, 15)
    YB[...] = z_chain(4, b_terms, BLs, BLr, BSs, BSr, "B")
    Y1s[...] = YB[yf2].astype(bf16)
    Yss[...] = YB[yb1].astype(bf16)
    send(Y1s, Y1r, ("Y1",), y_b)
    send(Yss, Ysr, ("Ys",), y_f)
    a_final(2)
    arrived(Y1r, ("Y1",))
    Y2s[...] = (YB[yf1] + Y1r[...].astype(f32)).astype(bf16)
    send(Y2s, Y2r, ("Y2",), y_b)
    a_final(3)
    arrived(Ysr, ("Ys",))
    arrived(Y2r, ("Y2",))
    FB[...] = (YB[y] + Ysr[...].astype(f32) + Y2r[...].astype(f32)).astype(bf16)
    FA[...] = a_final(4).astype(bf16)

    backs = []
    for j in range(2):
        for src, dst, name in ((FA, OA, "OA"), (FB, OB, "OB")):
            i = sent[0]
            sent[0] += 1
            first = rid((name, 0))
            second = rid((name, 1))
            base = keys[(name, 0)]
            backs.append((j, pltpu.make_async_remote_copy(src, dst.at[core], ssem.at[i], rsem.at[base + core], device_id=sources[j])))
    for j, c in backs:

        @pl.when(jnp.logical_not(loops & (j == x % 2)))
        def _():
            c.start()

    @pl.when(loops)
    def _():
        OA[core] = FA[...]
        OB[core] = FB[...]

    for c in range(2):

        @pl.when(jnp.logical_not(loops & (core == c)))
        def _():
            arrived(OA.at[c], ("OA", c))
            arrived(OB.at[c], ("OB", c))

    a0, a1 = OA[0].astype(f32), OA[1].astype(f32)

    @pl.when(ylo == 0)
    def _():
        gin[...] = jnp.concatenate([a0, a1[:8]], 0).astype(bf16)

    @pl.when(ylo == 1)
    def _():
        last = jnp.concatenate([OB[0].astype(f32), OB[1].astype(f32)[:, 2 * BW - D4:]], 1)
        gin[...] = jnp.concatenate([a1[8:], last], 0).astype(bf16)

    for c in range(2):

        @pl.when(jnp.logical_not(loops & (core == c)))
        def _():
            swaps[c].wait_send()

    for j, c in backs:

        @pl.when(jnp.logical_not(loops & (j == x % 2)))
        def _():
            c.wait_send()

    for c in sends:
        c.wait_send()
    assert sent[0] <= N_SEND and len(keys) <= N_RECV, (sent, len(keys))


def shards(inputs, levels, block_scales, grad_hidden):
    vm = lambda *shape: pltpu.VMEM(shape, bf16)
    vf = lambda *shape: pltpu.VMEM(shape, f32)
    vmem, smem = pl.BlockSpec(memory_space=pltpu.VMEM), pl.BlockSpec(memory_space=pltpu.SMEM)
    a_buf = vm(NZ, U, D4)
    y_buf = vm(U, BW)
    hidden, grad_inputs, grad_weight = pl.pallas_call(
        kernel,
        out_shape=(
            jax.ShapeDtypeStruct((NZ, ROWS, H), bf16),
            jax.ShapeDtypeStruct((24, D4), bf16),
            jax.ShapeDtypeStruct((D4, H), bf16),
        ),
        in_specs=[vmem, vmem, smem, vmem],
        out_specs=(vmem, vmem, vmem),
        scratch_shapes=[
            vm(D4, H),
            vm(32, D4), vm(2, 32, D4),
            vm(NY, NZ, ROWS, D4),
            vm(NY, NZ, ROWS, H), vm(NX - 1, NZ, ROWS, H), vm(NY, NZ, ROWS, H),
            vm(NY, NZ, ROWS, D4), vm(NY, NZ, U, D4), vm(NY, NZ, U, BW),
            a_buf, a_buf, a_buf, a_buf, a_buf, a_buf, vf(NZ, U, D4),
            vm(4, U, D4), vm(4, U, D4), vm(3, U, D4), vm(3, U, D4),
            vm(4, NY, U, BW), vm(4, NY, U, BW), vm(3, NY, U, BW), vm(3, NY, U, BW), vf(NY, U, BW),
            y_buf, y_buf, y_buf, y_buf, y_buf, y_buf,
            vm(U, D4), y_buf, vm(2, U, D4), vm(2, U, BW),
            pltpu.SemaphoreType.DMA((N_SEND,)),
            pltpu.SemaphoreType.DMA((N_RECV,)),
        ],
        compiler_params=pltpu.CompilerParams(
            collective_id=0, has_side_effects=True, vmem_limit_bytes=60 * 2**20
        ),
        name="grid_layer",
    )(inputs[0], levels, block_scales, grad_hidden.reshape(NZ, ROWS, H))
    return (hidden.reshape(grad_hidden.shape), grad_inputs[None], grad_weight)


def solution(mesh):
    placed = (
        P("dp", "row", "col"),
        P("row", ("dp", "col")),
        P("row", ("dp", "col")),
        P(None, "row", ("dp", "col")),
    )
    return jax.shard_map(
        shards,
        mesh=mesh,
        in_specs=placed,
        out_specs=(P(None, "row", ("dp", "col")), P("dp", "row", "col"), P("row", ("dp", "col"))),
        check_vma=False,
    )
```

time: 514 us -> 132 us (0.26)
  waiting for transfers between devices: 445 us -> 0 us
  Pallas kernels: 0 us -> 122 us
  starting transfers between devices: 20.6 us -> 0 us
  matrix products: 16.8 us -> 0 us
  between operations: 13.9 us -> 0.64 us
  local copies, waits for them, and re-layouts: 15.9 us -> 7.61 us
    unnamed x5 -> x0, waiting for transfers between devices: 265 us -> none
    all_gather x2 -> x0, waiting for transfers between devices: 148 us -> none  [the longest x1 118 us: shards(): lax.all_gather(mine, ('dp', 'col'), axis=0, tiled=False)]
    pallas_call x0 -> x1, Pallas kernels: none -> 122 us  [shards(): pl.pallas_call(kernel, out_shape=(jax.ShapeDtypeStruct((NZ, ROWS, H), bf1...]
    reduce_scatter x1 -> x0, waiting for transfers between devices: 26.3 us -> none  [shards(): lax.psum_scatter(part, 'row', scatter_dimension=0, tiled=True)]
    ppermute x2 -> x0, starting transfers between devices: 20.5 us -> none  [swap_row_col(): lax.ppermute(x, ('row', 'col'), [(r * n + c, c * n + r) for r in range(n)...]
    dot_general x3 -> x0, matrix products: 16.8 us -> none  [the longest x1 6.67 us: shards(): lax.dot_general(all_grad, weight, (((1,), (1,)), ((), ())), preferred_ele...]
    ppermute x2 -> x0, waiting for transfers between devices: 6.16 us -> none  [swap_row_col(): lax.ppermute(x, ('row', 'col'), [(r * n + c, c * n + r) for r in range(n)...]
    transpose x2 -> x0, local copies, waits for them, and re-layouts: 6.1 us -> none  [the longest x1 3.11 us: shards(): tok_rows.transpose(1, 0, 2, 3).reshape(n * replicas * block_tokens, feats)]
  transfers between devices with their start and end apart: 6 -> 0, of which waited for: 5 -> 0; matrix products, arithmetic and copies ran while one was open for 2% -> 0% of each run, Pallas kernels for 0% -> 0%
where the time goes in v2:
time: 132 us; the launch traced here: 130 us
  Pallas kernels  122 us (92%)
  local copies, waits for them, and re-layouts  7.61 us (6%)
    pallas_call x1, Pallas kernels, shards(): pl.pallas_call(kernel, out_shape=(jax.ShapeDtypeStruct((NZ, ROWS, H), bf1...  122 us
    unnamed x4, local copies, waits for them, and re-layouts  7.61 us

profile of v2, /device:TPU:17, one launch (start us, length us, event | category | flops | bytes accessed | tf_op | source)
XLA Modules:
  0.0 130.2 jit_solution(16417864363407831567)
XLA Ops:
  0.6 1.4 %copy.7.scl = f32[15,4]{1,0:T(8,128)} copy(f32[15,4]{0,1:T(4,128)} %param.6) | data formatting | bytes 480 | tf_op args[2]
  2.0 122.0 %grid_layer.1 = (bf16[8,48,512]{2,1,0:T(8,128)(2,1)}, bf16[24,1920]{1,0:T(8,128)(2,1)}, bf16[1920,512]{1,0:T(8,128)(2,1)}) custom-call(bf16[24,1920]{1,0:T(8,128)(2,1)} %bitcast.7, bf16[1920,512]{1,0:T(8,128)(2,1)} %lev.1, f32[15,4]{1,0:T(8,128)} %copy.7.scl, bf16[8,48,512]{2,1,0:T(8,128)(2,1)} %bitcast.5), custom_call_target="tpu_custom_call" | custom-call | tf_op jit(solution)/shard_map/grid_layer/pallas_call | solution.py:466
  124.0 1.8 %copy.11 = bf16[16,24,512]{2,1,0:T(8,128)(2,1)} copy(bf16[16,24,512]{2,1,0:T(8,128)(2,1)} %bitcast.4) | data formatting | bytes 786432
  125.8 1.5 %copy.12 = bf16[1,24,1920]{2,1,0:T(8,128)(2,1)} copy(bf16[1,24,1920]{2,1,0:T(8,128)(2,1)} %bitcast.6) | data formatting | bytes 184320
  127.3 2.9 %copy.13 = bf16[1920,512]{1,0:T(8,128)(2,1)} copy(bf16[1920,512]{1,0:T(8,128)(2,1)} %get-tuple-element.14) | data formatting | bytes 3932160

commit v3 on v1

v3 whole, which is shorter than its diff:
```python
import jax
import jax.numpy as jnp
from jax import lax
from jax.experimental import pallas as pl
from jax.experimental.pallas import tpu as pltpu
from jax.sharding import PartitionSpec as P

inv_root_two = 0.7071067811865476
inv_root_two_pi = 0.3989422804014327
bf16, f32 = jnp.bfloat16, jnp.float32

NZ, NY, NX = 8, 4, 4
ROWS = 48
U = 16
D4 = 1920
H = 512
BW = 1024
BO = 896
GROUPS = ((0, 1), (1, 3), (3, 5), (5, 7), (7, 8))
NEAR = 3
DIRECT = 4
N_SEND, N_RECV = 208, 208


def pos_f(k):
    return 0 if k == 0 else 2 * k - 1


def pos_b(k):
    return 2 * k


def sib_pos(p):
    if p == 0 or p == 7:
        return p
    return p + 1 if p % 2 else p - 1


def gelu_pair(pre):
    normal_cdf = 0.5 * (1.0 + lax.erf(pre * inv_root_two))
    density = jnp.exp(-0.5 * pre * pre) * inv_root_two_pi
    return (pre * normal_cdf, normal_cdf + pre * density)


def kernel(inp, lev, scl, gh, hid, gin, gw,
           L, W, S0, R0, X, GH, HD, PS, PR, PM, GP, GI, GA, GW, CA, CB,
           A1s, Ass, A2s, A1r, Asr, A2r, YA,
           ZLs, ZLr, ZSs, ZSr, BLs, BLr, BSs, BSr, YB,
           Y1s, Yss, Y2s, Y1r, Ysr, Y2r, FA, FB, OA, OB,
           ssem, rsem, lsem):
    dp, x, col = lax.axis_index("dp"), lax.axis_index("row"), lax.axis_index("col")
    z, ylo, yhi, core = dp // 2, dp % 2, col // 2, col % 2
    y = 2 * yhi + ylo
    s = 1 - 2 * core

    def dev(zz, yy, xx, cc):
        return {"dp": zz * 2 + yy % 2, "row": xx, "col": (yy // 2) * 2 + cc}

    sources = [dev(z, 2 * (x // 2) + j, y, x % 2) for j in range(2)]
    targets = [dev(z, x, 2 * yhi + core, c) for c in range(2)]
    loops = (x == y) & (core == x % 2)
    z_f, z_b = dev((z + s + NZ) % NZ, y, x, core), dev((z - s + NZ) % NZ, y, x, core)
    y_f, y_b = dev(z, (y + s + NY) % NY, x, core), dev(z, (y - s + NY) % NY, x, core)
    sib = dev(z, y, x, 1 - core)
    y_2 = dev(z, (y + 2) % NY, x, core)
    x_f, x_b = dev(z, y, (x + s + NX) % NX, core), dev(z, y, (x - s + NX) % NX, core)
    x_2 = dev(z, y, (x + 2) % NX, core)
    xf1, xb1, xf2 = (x - s + NX) % NX, (x + s + NX) % NX, (x + 2) % NX
    yf1, yb1, yf2 = (y - s + NY) % NY, (y + s + NY) % NY, (y + 2) % NY

    sends, keys, sent = [], {}, [0]

    def rid(key):
        if key not in keys:
            keys[key] = len(keys)
        return rsem.at[keys[key]]

    def copy(src, dst, key, to):
        i = sent[0]
        sent[0] += 1
        return pltpu.make_async_remote_copy(src, dst, ssem.at[i], rid(key), device_id=to)

    def send(src, dst, key, to):
        c = copy(src, dst, key, to)
        c.start()
        sends.append(c)

    def arrived(dst, key):
        pltpu.make_async_remote_copy(dst, dst, ssem.at[0], rid(key), device_id=sib).wait_recv()

    lev_in = pltpu.make_async_copy(lev, L, lsem.at[0])
    gh_in = pltpu.make_async_copy(gh, GH, lsem.at[1])
    lev_in.start()
    gh_in.start()
    bar = pltpu.get_barrier_semaphore()
    partners = sources + targets + [x_f, x_b, x_2, z_f, z_b, y_f, y_b, y_2, sib]
    for d in partners:
        pl.semaphore_signal(bar, 1, device_id=d)
    block = inp[...].astype(f32)
    S0[...] = jnp.concatenate([block[:, :BW], block[:, BO:]], 0).astype(bf16)
    pl.semaphore_wait(bar, len(partners))

    rid(("swap",))
    i_swap = sent[0]
    sent[0] += 1
    to_chip = dev(z, x, 2 * yhi + core, ylo)
    swap = pltpu.make_async_remote_copy(S0, R0.at[ylo], ssem.at[i_swap], rid(("swap",)), device_id=to_chip)

    @pl.when(jnp.logical_not(loops))
    def _():
        swap.start()

    @pl.when(loops)
    def _():
        R0[core] = S0[...]

    def weights(a0, a1):
        @pl.loop(a0, a1)
        def _(a):
            r = pl.ds(pl.multiple_of(a * 128, 128), 128)
            for b in range(H // 128):
                cs = pl.ds(b * 128, 128)
                W[r, cs] = (L[r, cs].astype(f32) * scl[b, a]).astype(bf16)

    @pl.when(jnp.logical_not(loops))
    def _():
        arrived(R0.at[core], ("swap",))

    send(R0.at[core], R0.at[core], ("hand",), sib)
    lev_in.wait()
    weights(0, 8)
    arrived(R0.at[1 - core], ("hand",))
    pair = [jnp.concatenate([R0[j].astype(f32)[:24], R0[j].astype(f32)[24:, BW - BO:]], 1) for j in range(2)]
    X[y, 0] = jnp.concatenate(pair, 0).astype(bf16)

    r_mine = pl.ds(pl.multiple_of(core * U, U), U)
    r_other = pl.ds(pl.multiple_of((1 - core) * U, U), U)
    r_b = pl.ds(2 * U, U)
    c_mine = pl.ds(pl.multiple_of(core * BO, 128), BW)
    c_other = pl.ds(pl.multiple_of((1 - core) * BO, 128), BW)
    c_give = pl.ds(pl.multiple_of(core * BW, 128), BO)
    c_take = pl.ds(pl.multiple_of((1 - core) * BW, 128), BO)

    def a_unit(yq, p):
        return X.at[yq, p, r_mine]

    def b_unit(yq, p):
        return X.at[yq, p, r_b, c_mine]

    name_of = {id(y): "0", id(yf1): "f1", id(yb1): "b1", id(yf2): "f2"}

    def at_dist(k):
        return [0] if k == 0 else [pos_f(k)] + ([pos_b(k)] if k < 4 else [])

    def y_start(p):
        send(a_unit(y, p), a_unit(y, p), ("Ay", p, 1), y_f)
        send(a_unit(y, p), a_unit(y, p), ("Ay", p, -1), y_b)
        if p == 7:
            send(a_unit(y, p), a_unit(y, p), ("Ay", p, 2), y_2)

    def y_hop1(p):
        arrived(a_unit(yf1, p), ("Ay", p, 1))
        if p != 7:
            send(a_unit(yf1, p), a_unit(yf1, p), ("Ay", p, 2), y_f)
        if p == 0:
            send(a_unit(yf1, 0), a_unit(yf1, 0), ("As0", -1), sib)
        arrived(a_unit(yb1, p), ("Ay", p, -1))
        if p == 0:
            send(a_unit(yb1, 0), a_unit(yb1, 0), ("As0", 1), sib)

    def y_hop2(p):
        arrived(a_unit(yf2, p), ("Ay", p, 2))
        if p == 0:
            send(a_unit(yf2, 0), a_unit(yf2, 0), ("As0", 2), sib)
        else:
            send(X.at[:, p, r_mine], X.at[:, sib_pos(p), r_mine], ("As", sib_pos(p)), sib)

    def bz_send(yq, k):
        if k < 4:
            send(b_unit(yq, pos_f(k)), b_unit(yq, pos_f(k + 1)), ("Bz", name_of[id(yq)], pos_f(k + 1)), z_f)
        if k < 3:
            send(b_unit(yq, pos_b(k)), b_unit(yq, pos_b(k + 1)), ("Bz", name_of[id(yq)], pos_b(k + 1)), z_b)

    def bz_hop(yq, k):
        for p in at_dist(k):
            arrived(b_unit(yq, p), ("Bz", name_of[id(yq)], p))
        bz_send(yq, k)

    def b_give(k):
        for p in at_dist(k):
            send(X.at[:, p, r_b, c_give], X.at[:, sib_pos(p), r_b, c_give], ("Bs", sib_pos(p)), sib)

    def sib_wait(k):
        for p in at_dist(k):
            if p == 0:
                for q, yq in ((1, yf1), (-1, yb1), (2, yf2)):
                    arrived(X.at[yq, 0, r_other], ("As0", q))
                    arrived(X.at[yq, 0, r_b, c_take], ("Bs0", q))
            else:
                arrived(X.at[:, p, r_other], ("As", p))
                arrived(X.at[:, p, r_b, c_take], ("Bs", p))

    def az_send(k):
        if k < 4:
            send(a_unit(y, pos_f(k)), a_unit(y, pos_f(k + 1)), ("Az", pos_f(k + 1)), z_f)
        if k < 3:
            send(a_unit(y, pos_b(k)), a_unit(y, pos_b(k + 1)), ("Az", pos_b(k + 1)), z_b)

    def tick(k):
        if k == 0:
            az_send(0)
            for q, to in ((1, y_f), (-1, y_b), (2, y_2)):
                send(b_unit(y, 0), b_unit(y, 0), ("By", q), to)
            y_start(0)
            bz_send(y, 0)
            return
        if k <= 4:
            for p in at_dist(k):
                arrived(a_unit(y, p), ("Az", p))
            az_send(k)
            for p in at_dist(k):
                y_start(p)
        if k == 1:
            for q, yq, r in ((1, yf1, -1), (-1, yb1, 1), (2, yf2, 2)):
                arrived(b_unit(yq, 0), ("By", q))
                bz_send(yq, 0)
                send(X.at[yq, 0, r_b, c_give], X.at[yq, 0, r_b, c_give], ("Bs0", r), sib)
        if k <= 4:
            bz_hop(y, k)
        for p in at_dist(k - 1):
            y_hop1(p)
        if 2 <= k <= 5:
            for yq in (yf1, yb1, yf2):
                bz_hop(yq, k - 1)
            b_give(k - 1)
        if k >= 2:
            for p in at_dist(k - 2):
                y_hop2(p)
        if k == 5:
            y_hop2(7)

    def partial_pre(g):
        p0, p1 = GROUPS[g]
        m = (p1 - p0) * ROWS
        for h in range(0, H, 256):
            rows = X[:, p0:p1].reshape(NY * m, D4)
            part = jnp.dot(rows, W[:, h:h + 256], preferred_element_type=f32)
            PS[:, p0:p1, :, h:h + 256] = part.astype(bf16).reshape(NY, p1 - p0, ROWS, 256)
        send(PS.at[xf2, p0:p1], PR.at[0, p0:p1], ("pre", g, 0), x_2 if g >= DIRECT else x_b)
        send(PS.at[xb1, p0:p1], PR.at[1, p0:p1], ("pre", g, 1), x_f)
        if g >= DIRECT:
            send(PS.at[xf1, p0:p1], PR.at[2, p0:p1], ("pre", g, 2), x_b)

    def pre_middle(g):
        p0, p1 = GROUPS[g]
        arrived(PR.at[0, p0:p1], ("pre", g, 0))
        PM[p0:p1] = (PS[xf1, p0:p1].astype(f32) + PR[0, p0:p1].astype(f32)).astype(bf16)
        send(PM.at[p0:p1], PR.at[2, p0:p1], ("pre", g, 2), x_b)

    def activate(g):
        p0, p1 = GROUPS[g]
        parts = (0, 1, 2) if g >= DIRECT else (1, 2)
        for d in parts:
            arrived(PR.at[d, p0:p1], ("pre", g, d))

        @pl.loop(p0, p1)
        def _(p):
            k = (p + 1) // 2
            zz = (z + (1 - 2 * (p % 2)) * k * s + NZ) % NZ
            pre = PS[x, p].astype(f32)
            for d in parts:
                pre += PR[d, p].astype(f32)
            activated, slope = gelu_pair(pre)
            HD[zz] = activated.astype(bf16)
            GP[x, p] = (GH[zz].astype(f32) * slope).astype(bf16)

        own = GP.at[x, p0:p1]
        send(own, own, ("gp", g, 1), x_f)
        send(own, own, ("gp", g, -1), x_b)
        if g >= DIRECT:
            send(own, own, ("gp", g, 2), x_2)

    def grad_middle(g):
        p0, p1 = GROUPS[g]
        arrived(GP.at[xf1, p0:p1], ("gp", g, 1))
        send(GP.at[xf1, p0:p1], GP.at[xf1, p0:p1], ("gp", g, 2), x_f)

    def input_terms(g):
        p0, p1 = GROUPS[g]
        m = (p1 - p0) * ROWS
        if g >= DIRECT:
            arrived(GP.at[xf1, p0:p1], ("gp", g, 1))
        arrived(GP.at[xb1, p0:p1], ("gp", g, -1))
        arrived(GP.at[xf2, p0:p1], ("gp", g, 2))

        @pl.loop(0, D4 // 384)
        def _(n):
            cs = pl.ds(pl.multiple_of(n * 384, 128), 384)
            rows = GP[:, p0:p1].reshape(NY * m, H)
            part = lax.dot_general(rows, W[cs, :], (((1,), (1,)), ((), ())), preferred_element_type=f32)
            GI[:, p0:p1, :, cs] = part.astype(bf16).reshape(NY, p1 - p0, ROWS, 384)

        for p in reversed(range(p0, p1)):
            q = sib_pos(p)
            send(GI.at[:, p, r_b, c_other], CB.at[:, q], ("CB", q), sib)
            send(GI.at[:, p, r_other], CA.at[:, q], ("CA", q), sib)

    def a_term(yq, p):
        return GI[yq, p, r_mine].astype(f32) + CA[yq, p].astype(f32)

    def ay_begin(p):
        arrived(CA.at[:, p], ("CA", p))
        A1s[p] = a_term(yf2, p).astype(bf16)
        send(A1s.at[p], A1r.at[p], ("A1", p), y_2 if p == 7 else y_b)
        if p == 7:
            A2s[p] = a_term(yf1, p).astype(bf16)
            send(A2s.at[p], A2r.at[p], ("A2", p), y_b)
        Ass[p] = a_term(yb1, p).astype(bf16)
        send(Ass.at[p], Asr.at[p], ("As_", p), y_f)

    def ay_middle(p):
        arrived(A1r.at[p], ("A1", p))
        A2s[p] = (a_term(yf1, p) + A1r[p].astype(f32)).astype(bf16)
        send(A2s.at[p], A2r.at[p], ("A2", p), y_b)

    def ay_end(p):
        arrived(Asr.at[p], ("As_", p))
        arrived(A2r.at[p], ("A2", p))
        total = a_term(y, p) + Asr[p].astype(f32) + A2r[p].astype(f32)
        if p == 7:
            arrived(A1r.at[p], ("A1", p))
            total += A1r[p].astype(f32)
        YA[p] = total

    def z_chain(j, term, at, ls, lr, ss, sr, name):
        if j == 0:
            at(ls, 0)[...] = term(pos_f(4)).astype(bf16)
        else:
            arrived(at(lr, j - 1), (name, "L", j))
            if j < 4:
                at(ls, j)[...] = (term(pos_f(4 - j)) + at(lr, j - 1)[...].astype(f32)).astype(bf16)
        if j < 4:
            send(at(ls, j), at(lr, j), (name, "L", j + 1), z_b)
        if j == 0:
            at(ss, 0)[...] = term(pos_b(3)).astype(bf16)
        elif j < 4:
            arrived(at(sr, j - 1), (name, "S", j))
            if j < 3:
                at(ss, j)[...] = (term(pos_b(3 - j)) + at(sr, j - 1)[...].astype(f32)).astype(bf16)
        if j < 3:
            send(at(ss, j), at(sr, j), (name, "S", j + 1), z_f)
        if j == 4:
            return term(0) + at(lr, 3)[...].astype(f32) + at(sr, 2)[...].astype(f32)

    outs = []

    def start_out(c):
        c.start()
        outs.append(c)

    def hidden_out():
        start_out(pltpu.make_async_copy(HD, hid, lsem.at[2]))

    def weight_tile(n, p0, p1):
        cs = pl.ds(pl.multiple_of(n * 128, 128), 128)
        rows = X[:, p0:p1, :, cs].reshape(NY * (p1 - p0) * ROWS, 128)
        grads = GP[:, p0:p1].reshape(NY * (p1 - p0) * ROWS, H)
        return cs, lax.dot_general(rows, grads, (((0,), (0,)), ((), ())), preferred_element_type=f32)

    def weight_far(n0, n1):
        @pl.loop(n0, n1)
        def _(n):
            cs, part = weight_tile(n, NEAR, NZ)
            GA[cs, :] = part

    def weight_grad(n0, n1):
        @pl.loop(n0, n1)
        def _(n):
            cs, part = weight_tile(n, 0, NEAR)
            GW[cs, :] = (GA[cs, :] + part).astype(bf16)

        r = pl.ds(n0 * 128, (n1 - n0) * 128)
        start_out(pltpu.make_async_copy(GW.at[r], gw.at[r], lsem.at[3 + n0]))

    def b_step(j, *rows):
        for yq in rows:
            nm = name_of[id(yq)]
            last = z_chain(
                j,
                lambda p: GI[yq, p, r_b, c_mine].astype(f32) + CB[yq, p].astype(f32),
                lambda buf, i: buf.at[i, yq],
                BLs, BLr, BSs, BSr, "B" + nm,
            )
            if j < 4:
                continue
            YB[yq] = last
            if nm == "f2":
                Y1s[...] = last.astype(bf16)
                send(Y1s, Y1r, ("Y1",), y_2)
            elif nm == "f1":
                Y2s[...] = last.astype(bf16)
                send(Y2s, Y2r, ("Y2",), y_b)
            elif nm == "b1":
                Yss[...] = last.astype(bf16)
                send(Yss, Ysr, ("Ys",), y_f)

    def b_end():
        arrived(Ysr, ("Ys",))
        arrived(Y2r, ("Y2",))
        arrived(Y1r, ("Y1",))
        FB[...] = (YB[y] + Ysr[...].astype(f32) + Y2r[...].astype(f32) + Y1r[...].astype(f32)).astype(bf16)

    def cb_wait(*ps):
        for p in ps:
            arrived(CB.at[:, p], ("CB", p))

    def a_step(j):
        last = z_chain(j, lambda p: YA[p], lambda buf, i: buf.at[i], ZLs, ZLr, ZSs, ZSr, "A")
        if j == 4:
            FA[...] = last.astype(bf16)

    backs = []

    def give_back():
        always = core >= 0
        for j, src, dst, name, which in ((0, FA, OA, "OA", always), (1, FA, OA, "OA", core == 1), (1, FB, OB, "OB", always)):
            i = sent[0]
            sent[0] += 1
            rid((name, 0))
            rid((name, 1))
            sem = rsem.at[keys[(name, 0)] + core]
            which = which & jnp.logical_not(loops & (j == x % 2))
            backs.append((which, pltpu.make_async_remote_copy(src, dst.at[core], ssem.at[i], sem, device_id=sources[j])))
        for which, c in backs:

            @pl.when(which)
            def _():
                c.start()

        @pl.when(loops)
        def _():
            OA[core] = FA[...]
            OB[core] = FB[...]

    def take_back():
        for c in range(2):
            far = jnp.logical_not(loops & (core == c))

            @pl.when(far if c == 1 else far & (ylo == 0))
            def _():
                arrived(OA.at[c], ("OA", c))

            @pl.when(far & (ylo == 1))
            def _():
                arrived(OB.at[c], ("OB", c))

        a1 = OA[1].astype(f32)

        @pl.when(ylo == 0)
        def _():
            gin[...] = jnp.concatenate([OA[0].astype(f32), a1[:8]], 0).astype(bf16)

        @pl.when(ylo == 1)
        def _():
            last = jnp.concatenate([OB[0].astype(f32), OB[1].astype(f32)[:, 2 * BW - D4:]], 1)
            gin[...] = jnp.concatenate([a1[8:], last], 0).astype(bf16)

    steps = [
        (tick, 0), (weights, 8, 15), (gh_in.wait,),
        (tick, 1), (tick, 2),
        (sib_wait, 0), (partial_pre, 0),
        (tick, 3), (pre_middle, 0), (sib_wait, 1), (partial_pre, 1),
        (tick, 4), (activate, 0), (pre_middle, 1), (sib_wait, 2), (partial_pre, 2),
        (tick, 5), (grad_middle, 0), (pre_middle, 2),
        (sib_wait, 3), (partial_pre, 3), (sib_wait, 4), (partial_pre, 4),
        (input_terms, 0), (activate, 2), (pre_middle, 3), (activate, 4), (grad_middle, 2),
        (ay_begin, 0), (activate, 3), (activate, 1), (hidden_out,),
        (input_terms, 4), (grad_middle, 3), (ay_middle, 0),
        (input_terms, 2), (grad_middle, 1),
        (ay_begin, 7), (ay_begin, 3), (ay_begin, 4),
        (input_terms, 3),
        (ay_end, 0), (cb_wait, 7, 6, 5),
        (b_step, 0, yf2, yf1, yb1, y),
        (ay_begin, 5), (ay_begin, 6), (ay_end, 7), (ay_middle, 3), (ay_middle, 4),
        (weight_far, 0, 4),
        (input_terms, 1),
        (cb_wait, 4, 3),
        (b_step, 1, yf2, yf1, yb1, y),
        (ay_middle, 5), (ay_middle, 6), (ay_end, 3), (ay_end, 4),
        (weight_far, 4, 7),
        (cb_wait, 2, 1, 0),
        (ay_begin, 2), (ay_begin, 1),
        (b_step, 2, yf2, yf1, yb1, y),
        (ay_end, 6), (a_step, 0), (ay_end, 5),
        (weight_far, 7, 11),
        (ay_middle, 2), (ay_middle, 1),
        (a_step, 1),
        (b_step, 3, yf2, yf1, yb1, y),
        (weight_far, 11, 15),
        (ay_end, 2), (a_step, 2), (ay_end, 1),
        (b_step, 4, yf2, yf1, yb1, y),
        (weight_grad, 0, 4),
        (a_step, 3),
        (weight_grad, 4, 8),
        (b_end,),
        (a_step, 4),
        (give_back,),
        (weight_grad, 8, 15),
        (take_back,),
    ]
    for step, *args in steps:
        step(*args)

    @pl.when(jnp.logical_not(loops))
    def _():
        swap.wait_send()

    for which, c in backs:

        @pl.when(which)
        def _():
            c.wait_send()

    for c in sends:
        c.wait_send()
    for c in outs:
        c.wait()
    assert sent[0] <= N_SEND and len(keys) <= N_RECV, (sent, len(keys))


def flush(h, i, w, ho, io, wo, sem):
    cut = [pl.ds(n * (D4 // 4), D4 // 4) for n in range(4)]
    parts = [(w.at[r], wo.at[r]) for r in cut] + [(h, ho), (i, io)]
    copies = [pltpu.make_async_copy(a, o, sem.at[n]) for n, (a, o) in enumerate(parts)]
    for c in copies:
        c.start()
    for c in copies:
        c.wait()


def shards(inputs, levels, block_scales, grad_hidden):
    vm = lambda *shape: pltpu.VMEM(shape, bf16)
    vf = lambda *shape: pltpu.VMEM(shape, f32)
    vmem, smem = pl.BlockSpec(memory_space=pltpu.VMEM), pl.BlockSpec(memory_space=pltpu.SMEM)
    hbm, far = pl.BlockSpec(memory_space=pl.ANY), pl.BlockSpec(memory_space=pltpu.HBM)
    stay = lambda a: pltpu.with_memory_space_constraint(a, pltpu.HBM)
    a_buf = vm(NZ, U, D4)
    y_buf = vm(U, BW)
    out_shape = (
        jax.ShapeDtypeStruct((NZ, ROWS, H), bf16),
        jax.ShapeDtypeStruct((24, D4), bf16),
        jax.ShapeDtypeStruct((D4, H), bf16),
    )
    outs = pl.pallas_call(
        kernel,
        out_shape=out_shape,
        in_specs=[vmem, far, smem, far],
        out_specs=(hbm, vmem, hbm),
        scratch_shapes=[
            vm(D4, H), vm(D4, H),
            vm(ROWS, BW), vm(2, ROWS, BW),
            vm(NY, NZ, ROWS, D4),
            vm(NZ, ROWS, H), vm(NZ, ROWS, H),
            vm(NY, NZ, ROWS, H), vm(NX - 1, NZ, ROWS, H), vm(NZ, ROWS, H), vm(NY, NZ, ROWS, H),
            vm(NY, NZ, ROWS, D4), vf(D4, H), vm(D4, H),
            vm(NY, NZ, U, D4), vm(NY, NZ, U, BW),
            a_buf, a_buf, a_buf, a_buf, a_buf, a_buf, vf(NZ, U, D4),
            vm(4, U, D4), vm(4, U, D4), vm(3, U, D4), vm(3, U, D4),
            vm(4, NY, U, BW), vm(4, NY, U, BW), vm(3, NY, U, BW), vm(3, NY, U, BW), vf(NY, U, BW),
            y_buf, y_buf, y_buf, y_buf, y_buf, y_buf,
            vm(U, D4), y_buf, vm(2, U, D4), vm(2, U, BW),
            pltpu.SemaphoreType.DMA((N_SEND,)),
            pltpu.SemaphoreType.DMA((N_RECV,)),
            pltpu.SemaphoreType.DMA((20,)),
        ],
        compiler_params=pltpu.CompilerParams(
            collective_id=0, has_side_effects=True, vmem_limit_bytes=46 * 2**20
        ),
        name="grid_layer",
    )(inputs[0], stay(levels), block_scales.T, stay(grad_hidden.reshape(NZ, ROWS, H)))
    hidden, grad_inputs, grad_weight = pl.pallas_call(
        flush,
        out_shape=out_shape,
        in_specs=[hbm] * 3,
        out_specs=(hbm,) * 3,
        scratch_shapes=[pltpu.SemaphoreType.DMA((6,))],
        compiler_params=pltpu.CompilerParams(vmem_limit_bytes=2**20),
        name="flush",
    )(*outs)
    return (hidden.reshape(grad_hidden.shape), grad_inputs[None], grad_weight)


def solution(mesh):
    placed = (
        P("dp", "row", "col"),
        P("row", ("dp", "col")),
        P("row", ("dp", "col")),
        P(None, "row", ("dp", "col")),
    )
    return jax.shard_map(
        shards,
        mesh=mesh,
        in_specs=placed,
        out_specs=(P(None, "row", ("dp", "col")), P("dp", "row", "col"), P("row", ("dp", "col"))),
        check_vma=False,
    )
```

time: 514 us -> 107 us (0.21)
  waiting for transfers between devices: 445 us -> 0 us
  Pallas kernels: 0 us -> 104 us
  starting transfers between devices: 20.6 us -> 0 us
  matrix products: 16.8 us -> 0 us
  local copies, waits for them, and re-layouts: 15.9 us -> 1.56 us
  between operations: 13.9 us -> 0.65 us
    unnamed x5 -> x0, waiting for transfers between devices: 265 us -> none
    all_gather x2 -> x0, waiting for transfers between devices: 148 us -> none  [the longest x1 118 us: shards(): lax.all_gather(mine, ('dp', 'col'), axis=0, tiled=False)]
    pallas_call x0 -> x2, Pallas kernels: none -> 104 us  [the longest x1 103 us: shards(): pl.pallas_call(kernel, out_shape=out_shape, in_specs=[vmem, far, smem, fa...]
    reduce_scatter x1 -> x0, waiting for transfers between devices: 26.3 us -> none  [shards(): lax.psum_scatter(part, 'row', scatter_dimension=0, tiled=True)]
    ppermute x2 -> x0, starting transfers between devices: 20.5 us -> none  [swap_row_col(): lax.ppermute(x, ('row', 'col'), [(r * n + c, c * n + r) for r in range(n)...]
    dot_general x3 -> x0, matrix products: 16.8 us -> none  [the longest x1 6.67 us: shards(): lax.dot_general(all_grad, weight, (((1,), (1,)), ((), ())), preferred_ele...]
    unnamed x14 -> x4, local copies, waits for them, and re-layouts: 9.19 us -> 1.56 us
    ppermute x2 -> x0, waiting for transfers between devices: 6.16 us -> none  [swap_row_col(): lax.ppermute(x, ('row', 'col'), [(r * n + c, c * n + r) for r in range(n)...]
  transfers between devices with their start and end apart: 6 -> 0, of which waited for: 5 -> 0; matrix products, arithmetic and copies ran while one was open for 2% -> 0% of each run, Pallas kernels for 0% -> 0%
where the time goes in v3:
time: 107 us; the launch traced here: 106 us
  Pallas kernels  104 us (97%)
  local copies, waits for them, and re-layouts  1.56 us (1%)
    pallas_call x1, Pallas kernels, shards(): pl.pallas_call(kernel, out_shape=out_shape, in_specs=[vmem, far, smem, fa...  103 us

profile of v3, /device:TPU:17, one launch (start us, length us, event | category | flops | bytes accessed | tf_op | source)
XLA Modules:
  0.0 106.2 jit_solution(14286987722606331965)
XLA Ops:
  0.6 0.0 copy-start
  0.6 0.9 copy-done
  1.5 0.0 copy-start.1
  1.5 0.7 copy-done.1
  2.2 102.5 %grid_layer.1 = (bf16[8,48,512]{2,1,0:T(8,128)(2,1)S(1)}, bf16[24,1920]{1,0:T(8,128)(2,1)S(1)}, bf16[1920,512]{1,0:T(8,128)(2,1)S(1)}) custom-call(bf16[24,1920]{1,0:T(8,128)(2,1)S(1)} %bitcast.5, bf16[1920,512]{1,0:T(8,128)(2,1)} %lev.1, f32[4,15]{1,0:T(4,128)S(1)} %bitcast.6, bf16[8,48,512]{2,1,0:T(8,128)(2,1)} %bitcast.7), custom_call_target="tpu_custom_call" | custom-call | tf_op jit(solution)/shard_map/grid_layer/pallas_call | solution.py:554
  104.7 1.5 %flush.1 = (bf16[8,48,512]{2,1,0:T(8,128)(2,1)}, bf16[24,1920]{1,0:T(8,128)(2,1)}, bf16[1920,512]{1,0:T(8,128)(2,1)}) custom-call(bf16[8,48,512]{2,1,0:T(8,128)(2,1)S(1)} %get-tuple-element.9.h, bf16[24,1920]{1,0:T(8,128)(2,1)S(1)} %get-tuple-element.10.i, bf16[1920,512]{1,0:T(8,128)(2,1)S(1)} %get-tuple-element.11.w), custom_call_target="tpu_custom_call" | custom-call | tf_op jit(solution)/shard_map/flush/pallas_call | solution.py:581
Async XLA Ops:
  0.6 0.9 copy-start
  1.5 0.7 copy-start.1

commit v4 on v3

--- a/solution.py
+++ b/solution.py
@@ -42,8 +42,8 @@
     return (pre * normal_cdf, normal_cdf + pre * density)
 
 
-def kernel(inp, lev, scl, gh, hid, gin, gw,
-           L, W, S0, R0, X, GH, HD, PS, PR, PM, GP, GI, GA, GW, CA, CB,
+def kernel(inp, lev, scl_hbm, gh, hid, gin, gw,
+           B0, scl, L, W, WT, S0, R0, X, GH, HD, PS, PR, PM, GP, GI, GA, GW, CA, CB,
            A1s, Ass, A2s, A1r, Asr, A2r, YA,
            ZLs, ZLr, ZSs, ZSr, BLs, BLr, BSs, BSr, YB,
            Y1s, Yss, Y2s, Y1r, Ysr, Y2r, FA, FB, OA, OB,
@@ -88,15 +88,20 @@
     def arrived(dst, key):
         pltpu.make_async_remote_copy(dst, dst, ssem.at[0], rid(key), device_id=sib).wait_recv()
 
+    in_c = pltpu.make_async_copy(inp, B0, lsem.at[18])
+    scl_in = pltpu.make_async_copy(scl_hbm, scl, lsem.at[19])
     lev_in = pltpu.make_async_copy(lev, L, lsem.at[0])
     gh_in = pltpu.make_async_copy(gh, GH, lsem.at[1])
+    in_c.start()
+    scl_in.start()
     lev_in.start()
     gh_in.start()
     bar = pltpu.get_barrier_semaphore()
     partners = sources + targets + [x_f, x_b, x_2, z_f, z_b, y_f, y_b, y_2, sib]
     for d in partners:
         pl.semaphore_signal(bar, 1, device_id=d)
-    block = inp[...].astype(f32)
+    in_c.wait()
+    block = B0[...].astype(f32)
     S0[...] = jnp.concatenate([block[:, :BW], block[:, BO:]], 0).astype(bf16)
     pl.semaphore_wait(bar, len(partners))
 
@@ -120,22 +125,44 @@
             r = pl.ds(pl.multiple_of(a * 128, 128), 128)
             for b in range(H // 128):
                 cs = pl.ds(b * 128, 128)
-                W[r, cs] = (L[r, cs].astype(f32) * scl[b, a]).astype(bf16)
+                block = L[r, cs].astype(f32) * scl[b, a]
+                W[r, cs] = block.astype(bf16)
+                WT[cs, r] = block.T.astype(bf16)
 
     @pl.when(jnp.logical_not(loops))
     def _():
         arrived(R0.at[core], ("swap",))
 
     send(R0.at[core], R0.at[core], ("hand",), sib)
-    lev_in.wait()
-    weights(0, 8)
-    arrived(R0.at[1 - core], ("hand",))
-    pair = [jnp.concatenate([R0[j].astype(f32)[:24], R0[j].astype(f32)[24:, BW - BO:]], 1) for j in range(2)]
-    X[y, 0] = jnp.concatenate(pair, 0).astype(bf16)
-
-    r_mine = pl.ds(pl.multiple_of(core * U, U), U)
-    r_other = pl.ds(pl.multiple_of((1 - core) * U, U), U)
-    r_b = pl.ds(2 * U, U)
+
+    def unpacked(j):
+        both = R0[j].astype(f32)
+        return jnp.concatenate([both[:24], both[24:, BW - BO:]], 1)
+
+    def put_a(c):
+        X[y, 0, 2 * U * c:2 * U * c + U] = unpacked(c)[8 * c:8 * c + U].astype(bf16)
+
+    for c in range(2):
+
+        @pl.when(core == c)
+        def _():
+            put_a(c)
+
+    def rest():
+        scl_in.wait()
+        lev_in.wait()
+        weights(0, 5)
+        arrived(R0.at[1 - core], ("hand",))
+        X[y, 0, U:2 * U] = jnp.concatenate([unpacked(0)[U:], unpacked(1)[:8]], 0).astype(bf16)
+        for c in range(2):
+
+            @pl.when(core == 1 - c)
+            def _():
+                put_a(c)
+
+    r_mine = pl.ds(pl.multiple_of(core * 2 * U, U), U)
+    r_other = pl.ds(pl.multiple_of((1 - core) * 2 * U, U), U)
+    r_b = pl.ds(U, U)
     c_mine = pl.ds(pl.multiple_of(core * BO, 128), BW)
     c_other = pl.ds(pl.multiple_of((1 - core) * BO, 128), BW)
     c_give = pl.ds(pl.multiple_of(core * BW, 128), BO)
@@ -209,9 +236,10 @@
     def tick(k):
         if k == 0:
             az_send(0)
+            y_start(0)
+            rest()
             for q, to in ((1, y_f), (-1, y_b), (2, y_2)):
                 send(b_unit(y, 0), b_unit(y, 0), ("By", q), to)
-            y_start(0)
             bz_send(y, 0)
             return
         if k <= 4:
@@ -297,7 +325,7 @@
         def _(n):
             cs = pl.ds(pl.multiple_of(n * 384, 128), 384)
             rows = GP[:, p0:p1].reshape(NY * m, H)
-            part = lax.dot_general(rows, W[cs, :], (((1,), (1,)), ((), ())), preferred_element_type=f32)
+            part = jnp.dot(rows, WT[:, cs], preferred_element_type=f32)
             GI[:, p0:p1, :, cs] = part.astype(bf16).reshape(NY, p1 - p0, ROWS, 384)
 
         for p in reversed(range(p0, p1)):
@@ -311,8 +339,8 @@
     def ay_begin(p):
         arrived(CA.at[:, p], ("CA", p))
         A1s[p] = a_term(yf2, p).astype(bf16)
-        send(A1s.at[p], A1r.at[p], ("A1", p), y_2 if p == 7 else y_b)
-        if p == 7:
+        send(A1s.at[p], A1r.at[p], ("A1", p), y_2 if p >= 5 else y_b)
+        if p >= 5:
             A2s[p] = a_term(yf1, p).astype(bf16)
             send(A2s.at[p], A2r.at[p], ("A2", p), y_b)
         Ass[p] = a_term(yb1, p).astype(bf16)
@@ -327,7 +355,7 @@
         arrived(Asr.at[p], ("As_", p))
         arrived(A2r.at[p], ("A2", p))
         total = a_term(y, p) + Asr[p].astype(f32) + A2r[p].astype(f32)
-        if p == 7:
+        if p >= 5:
             arrived(A1r.at[p], ("A1", p))
             total += A1r[p].astype(f32)
         YA[p] = total
@@ -420,17 +448,20 @@
             FA[...] = last.astype(bf16)
 
     backs = []
+    rid(("OB", 0))
+    rid(("OB", 1))
+    b_sems = keys[("OB", 0)]
 
     def give_back():
-        always = core >= 0
-        for j, src, dst, name, which in ((0, FA, OA, "OA", always), (1, FA, OA, "OA", core == 1), (1, FB, OB, "OB", always)):
-            i = sent[0]
-            sent[0] += 1
-            rid((name, 0))
-            rid((name, 1))
-            sem = rsem.at[keys[(name, 0)] + core]
-            which = which & jnp.logical_not(loops & (j == x % 2))
-            backs.append((which, pltpu.make_async_remote_copy(src, dst.at[core], ssem.at[i], sem, device_id=sources[j])))
+        for j in range(2):
+            other = jnp.logical_not(loops & (j == x % 2))
+            for src, dst, sem, which in (
+                (FA, OA, rid(("OA",)), other & (core == j)),
+                (FB, OB.at[core], rsem.at[b_sems + core], other),
+            ):
+                i = sent[0]
+                sent[0] += 1
+                backs.append((which, pltpu.make_async_remote_copy(src, dst, ssem.at[i], sem, device_id=sources[j])))
         for which, c in backs:
 
             @pl.when(which)
@@ -439,41 +470,40 @@
 
         @pl.when(loops)
         def _():
-            OA[core] = FA[...]
+            OA[...] = FA[...]
             OB[core] = FB[...]
 
     def take_back():
+        @pl.when(jnp.logical_not(loops))
+        def _():
+            arrived(OA, ("OA",))
+
         for c in range(2):
-            far = jnp.logical_not(loops & (core == c))
-
-            @pl.when(far if c == 1 else far & (ylo == 0))
-            def _():
-                arrived(OA.at[c], ("OA", c))
-
-            @pl.when(far & (ylo == 1))
+
+            @pl.when(jnp.logical_not(loops & (core == c)))
             def _():
                 arrived(OB.at[c], ("OB", c))
 
-        a1 = OA[1].astype(f32)
+        a_rows = OA[...].astype(f32)
+        b_rows = jnp.concatenate([OB[0].astype(f32), OB[1].astype(f32)[:, 2 * BW - D4:]], 1)
 
         @pl.when(ylo == 0)
         def _():
-            gin[...] = jnp.concatenate([OA[0].astype(f32), a1[:8]], 0).astype(bf16)
+            gin[...] = jnp.concatenate([a_rows, b_rows[:8]], 0).astype(bf16)
 
         @pl.when(ylo == 1)
         def _():
-            last = jnp.concatenate([OB[0].astype(f32), OB[1].astype(f32)[:, 2 * BW - D4:]], 1)
-            gin[...] = jnp.concatenate([a1[8:], last], 0).astype(bf16)
+            gin[...] = jnp.concatenate([b_rows[8:], a_rows], 0).astype(bf16)
 
     steps = [
-        (tick, 0), (weights, 8, 15), (gh_in.wait,),
+        (tick, 0), (weights, 5, 15), (gh_in.wait,),
         (tick, 1), (tick, 2),
         (sib_wait, 0), (partial_pre, 0),
         (tick, 3), (pre_middle, 0), (sib_wait, 1), (partial_pre, 1),
-        (tick, 4), (activate, 0), (pre_middle, 1), (sib_wait, 2), (partial_pre, 2),
-        (tick, 5), (grad_middle, 0), (pre_middle, 2),
+        (tick, 4), (activate, 0), (sib_wait, 2), (partial_pre, 2),
+        (tick, 5), (pre_middle, 1), (grad_middle, 0),
         (sib_wait, 3), (partial_pre, 3), (sib_wait, 4), (partial_pre, 4),
-        (input_terms, 0), (activate, 2), (pre_middle, 3), (activate, 4), (grad_middle, 2),
+        (pre_middle, 2), (input_terms, 0), (activate, 2), (pre_middle, 3), (activate, 4), (grad_middle, 2),
         (ay_begin, 0), (activate, 3), (activate, 1), (hidden_out,),
         (input_terms, 4), (grad_middle, 3), (ay_middle, 0),
         (input_terms, 2), (grad_middle, 1),
@@ -481,31 +511,28 @@
         (input_terms, 3),
         (ay_end, 0), (cb_wait, 7, 6, 5),
         (b_step, 0, yf2, yf1, yb1, y),
-        (ay_begin, 5), (ay_begin, 6), (ay_end, 7), (ay_middle, 3), (ay_middle, 4),
-        (weight_far, 0, 4),
+        (ay_begin, 6), (ay_begin, 5), (ay_end, 7), (ay_middle, 3), (ay_middle, 4),
         (input_terms, 1),
         (cb_wait, 4, 3),
         (b_step, 1, yf2, yf1, yb1, y),
-        (ay_middle, 5), (ay_middle, 6), (ay_end, 3), (ay_end, 4),
-        (weight_far, 4, 7),
-        (cb_wait, 2, 1, 0),
-        (ay_begin, 2), (ay_begin, 1),
+        (ay_end, 6), (a_step, 0), (ay_end, 5),
+        (cb_wait, 2, 1, 0), (ay_begin, 2), (ay_begin, 1), (ay_end, 4), (ay_end, 3),
+        (weight_far, 0, 3),
         (b_step, 2, yf2, yf1, yb1, y),
-        (ay_end, 6), (a_step, 0), (ay_end, 5),
-        (weight_far, 7, 11),
+        (a_step, 1),
+        (weight_far, 3, 6),
         (ay_middle, 2), (ay_middle, 1),
-        (a_step, 1),
         (b_step, 3, yf2, yf1, yb1, y),
-        (weight_far, 11, 15),
         (ay_end, 2), (a_step, 2), (ay_end, 1),
+        (weight_far, 6, 10),
         (b_step, 4, yf2, yf1, yb1, y),
-        (weight_grad, 0, 4),
+        (weight_far, 10, 12),
         (a_step, 3),
-        (weight_grad, 4, 8),
+        (weight_far, 12, 15), (weight_grad, 0, 5),
         (b_end,),
         (a_step, 4),
         (give_back,),
-        (weight_grad, 8, 15),
+        (weight_grad, 5, 15),
         (take_back,),
     ]
     for step, *args in steps:
@@ -541,7 +568,7 @@
 def shards(inputs, levels, block_scales, grad_hidden):
     vm = lambda *shape: pltpu.VMEM(shape, bf16)
     vf = lambda *shape: pltpu.VMEM(shape, f32)
-    vmem, smem = pl.BlockSpec(memory_space=pltpu.VMEM), pl.BlockSpec(memory_space=pltpu.SMEM)
+    vmem = pl.BlockSpec(memory_space=pltpu.VMEM)
     hbm, far = pl.BlockSpec(memory_space=pl.ANY), pl.BlockSpec(memory_space=pltpu.HBM)
     stay = lambda a: pltpu.with_memory_space_constraint(a, pltpu.HBM)
     a_buf = vm(NZ, U, D4)
@@ -554,10 +581,11 @@
     outs = pl.pallas_call(
         kernel,
         out_shape=out_shape,
-        in_specs=[vmem, far, smem, far],
+        in_specs=[far, far, far, far],
         out_specs=(hbm, vmem, hbm),
         scratch_shapes=[
-            vm(D4, H), vm(D4, H),
+            vm(24, D4), pltpu.SMEM((H // 128, D4 // 128), f32),
+            vm(D4, H), vm(D4, H), vm(H, D4),
             vm(ROWS, BW), vm(2, ROWS, BW),
             vm(NY, NZ, ROWS, D4),
             vm(NZ, ROWS, H), vm(NZ, ROWS, H),
@@ -568,16 +596,16 @@
             vm(4, U, D4), vm(4, U, D4), vm(3, U, D4), vm(3, U, D4),
             vm(4, NY, U, BW), vm(4, NY, U, BW), vm(3, NY, U, BW), vm(3, NY, U, BW), vf(NY, U, BW),
             y_buf, y_buf, y_buf, y_buf, y_buf, y_buf,
-            vm(U, D4), y_buf, vm(2, U, D4), vm(2, U, BW),
+            vm(U, D4), y_buf, vm(U, D4), vm(2, U, BW),
             pltpu.SemaphoreType.DMA((N_SEND,)),
             pltpu.SemaphoreType.DMA((N_RECV,)),
-            pltpu.SemaphoreType.DMA((20,)),
+            pltpu.SemaphoreType.DMA((24,)),
         ],
         compiler_params=pltpu.CompilerParams(
             collective_id=0, has_side_effects=True, vmem_limit_bytes=46 * 2**20
         ),
         name="grid_layer",
-    )(inputs[0], stay(levels), block_scales.T, stay(grad_hidden.reshape(NZ, ROWS, H)))
+    )(stay(inputs[0]), stay(levels), stay(block_scales.T), stay(grad_hidden.reshape(NZ, ROWS, H)))
     hidden, grad_inputs, grad_weight = pl.pallas_call(
         flush,
         out_shape=out_shape,

time: 107 us -> 103 us (0.963)
  Pallas kernels: 104 us -> 102 us
  local copies, waits for them, and re-layouts: 1.56 us -> 0 us
    pallas_call x1, Pallas kernels: 103 us -> 100 us  [shards(): pl.pallas_call(kernel, out_shape=out_shape, in_specs=[far, far, far, far]...]
    unnamed x4 -> x0, local copies, waits for them, and re-layouts: 1.56 us -> none
where the time goes in v4:
time: 103 us; the launch traced here: 102 us
  Pallas kernels  102 us (99%)
    pallas_call x1, Pallas kernels, shards(): pl.pallas_call(kernel, out_shape=out_shape, in_specs=[far, far, far, far]...  100 us

profile of v4, /device:TPU:17, one launch (start us, length us, event | category | flops | bytes accessed | tf_op | source)
XLA Modules:
  0.0 102.4 jit_solution(12680477133941050122)
XLA Ops:
  0.6 100.3 %grid_layer.1 = (bf16[8,48,512]{2,1,0:T(8,128)(2,1)S(1)}, bf16[24,1920]{1,0:T(8,128)(2,1)S(1)}, bf16[1920,512]{1,0:T(8,128)(2,1)S(1)}) custom-call(bf16[24,1920]{1,0:T(8,128)(2,1)} %bitcast.6, bf16[1920,512]{1,0:T(8,128)(2,1)} %lev.1, f32[4,15]{1,0:T(4,128)} %bitcast.7, bf16[8,48,512]{2,1,0:T(8,128)(2,1)} %bitcast.5), custom_call_target="tpu_custom_call" | custom-call | tf_op jit(solution)/shard_map/grid_layer/pallas_call | solution.py:581
  101.0 1.5 %flush.1 = (bf16[8,48,512]{2,1,0:T(8,128)(2,1)}, bf16[24,1920]{1,0:T(8,128)(2,1)}, bf16[1920,512]{1,0:T(8,128)(2,1)}) custom-call(bf16[8,48,512]{2,1,0:T(8,128)(2,1)S(1)} %get-tuple-element.9.h, bf16[24,1920]{1,0:T(8,128)(2,1)S(1)} %get-tuple-element.10.i, bf16[1920,512]{1,0:T(8,128)(2,1)S(1)} %get-tuple-element.11.w), custom_call_target="tpu_custom_call" | custom-call | tf_op jit(solution)/shard_map/flush/pallas_call | solution.py:609

commit v5 on v4

--- a/solution.py
+++ b/solution.py
@@ -43,7 +43,7 @@
 
 
 def kernel(inp, lev, scl_hbm, gh, hid, gin, gw,
-           B0, scl, L, W, WT, S0, R0, X, GH, HD, PS, PR, PM, GP, GI, GA, GW, CA, CB,
+           B0, scl, L, W, WT, SA, SB, RB, X, GH, HD, PS, PR, PM, GP, GI, GA, GW, CA, CB,
            A1s, Ass, A2s, A1r, Asr, A2r, YA,
            ZLs, ZLr, ZSs, ZSr, BLs, BLr, BSs, BSr, YB,
            Y1s, Yss, Y2s, Y1r, Ysr, Y2r, FA, FB, OA, OB,
@@ -102,22 +102,36 @@
         pl.semaphore_signal(bar, 1, device_id=d)
     in_c.wait()
     block = B0[...].astype(f32)
-    S0[...] = jnp.concatenate([block[:, :BW], block[:, BO:]], 0).astype(bf16)
+    for j in range(2):
+
+        @pl.when(ylo == j)
+        def _():
+            SA[...] = block[8 * j:8 * j + U].astype(bf16)
+            eight = block[U:] if j == 0 else block[:8]
+            SB[...] = jnp.concatenate([eight[:, :BW], eight[:, BO:]], 0).astype(bf16)
+
     pl.semaphore_wait(bar, len(partners))
 
-    rid(("swap",))
-    i_swap = sent[0]
-    sent[0] += 1
+    r_mine = pl.ds(pl.multiple_of(core * 2 * U, U), U)
+    r_other = pl.ds(pl.multiple_of((1 - core) * 2 * U, U), U)
+    r_b = pl.ds(U, U)
+
     to_chip = dev(z, x, 2 * yhi + core, ylo)
-    swap = pltpu.make_async_remote_copy(S0, R0.at[ylo], ssem.at[i_swap], rid(("swap",)), device_id=to_chip)
+    r_to = pl.ds(pl.multiple_of(ylo * 2 * U, U), U)
+    swaps = []
+    for src, dst, key in ((SA, X.at[x, 0, r_to], ("swap", 0)), (SB, RB.at[ylo], ("swap", 1))):
+        swaps.append(pltpu.make_async_remote_copy(src, dst, ssem.at[sent[0]], rid(key), device_id=to_chip))
+        sent[0] += 1
 
     @pl.when(jnp.logical_not(loops))
     def _():
-        swap.start()
+        for c in swaps:
+            c.start()
 
     @pl.when(loops)
     def _():
-        R0[core] = S0[...]
+        X[y, 0, r_mine] = SA[...]
+        RB[core] = SB[...]
 
     def weights(a0, a1):
         @pl.loop(a0, a1)
@@ -125,44 +139,36 @@
             r = pl.ds(pl.multiple_of(a * 128, 128), 128)
             for b in range(H // 128):
                 cs = pl.ds(b * 128, 128)
-                block = L[r, cs].astype(f32) * scl[b, a]
-                W[r, cs] = block.astype(bf16)
-                WT[cs, r] = block.T.astype(bf16)
+                W[r, cs] = (L[r, cs].astype(f32) * scl[b, a]).astype(bf16)
+
+    def transposes(a0, a1):
+        @pl.loop(a0, a1)
+        def _(a):
+            r = pl.ds(pl.multiple_of(a * 128, 128), 128)
+            for b in range(H // 128):
+                cs = pl.ds(b * 128, 128)
+                WT[cs, r] = W[r, cs].astype(f32).T.astype(bf16)
 
     @pl.when(jnp.logical_not(loops))
     def _():
-        arrived(R0.at[core], ("swap",))
-
-    send(R0.at[core], R0.at[core], ("hand",), sib)
-
-    def unpacked(j):
-        both = R0[j].astype(f32)
-        return jnp.concatenate([both[:24], both[24:, BW - BO:]], 1)
-
-    def put_a(c):
-        X[y, 0, 2 * U * c:2 * U * c + U] = unpacked(c)[8 * c:8 * c + U].astype(bf16)
-
-    for c in range(2):
-
-        @pl.when(core == c)
+        arrived(X.at[y, 0, r_mine], ("swap", 0))
+
+    def rest():
+        send(X.at[y, 0, r_mine], X.at[y, 0, r_mine], ("hand", 0), sib)
+
+        @pl.when(jnp.logical_not(loops))
         def _():
-            put_a(c)
-
-    def rest():
+            arrived(RB.at[core], ("swap", 1))
+
+        send(RB.at[core], RB.at[core], ("hand", 1), sib)
         scl_in.wait()
         lev_in.wait()
-        weights(0, 5)
-        arrived(R0.at[1 - core], ("hand",))
-        X[y, 0, U:2 * U] = jnp.concatenate([unpacked(0)[U:], unpacked(1)[:8]], 0).astype(bf16)
-        for c in range(2):
-
-            @pl.when(core == 1 - c)
-            def _():
-                put_a(c)
-
-    r_mine = pl.ds(pl.multiple_of(core * 2 * U, U), U)
-    r_other = pl.ds(pl.multiple_of((1 - core) * 2 * U, U), U)
-    r_b = pl.ds(U, U)
+        weights(0, 3)
+        arrived(RB.at[1 - core], ("hand", 1))
+        eights = [RB[j].astype(f32) for j in range(2)]
+        eights = [jnp.concatenate([v[:8], v[8:, BW - BO:]], 1) for v in eights]
+        X[y, 0, U:2 * U] = jnp.concatenate(eights, 0).astype(bf16)
+
     c_mine = pl.ds(pl.multiple_of(core * BO, 128), BW)
     c_other = pl.ds(pl.multiple_of((1 - core) * BO, 128), BW)
     c_give = pl.ds(pl.multiple_of(core * BW, 128), BO)
@@ -220,6 +226,7 @@
     def sib_wait(k):
         for p in at_dist(k):
             if p == 0:
+                arrived(X.at[y, 0, r_other], ("hand", 0))
                 for q, yq in ((1, yf1), (-1, yb1), (2, yf2)):
                     arrived(X.at[yq, 0, r_other], ("As0", q))
                     arrived(X.at[yq, 0, r_b, c_take], ("Bs0", q))
@@ -452,17 +459,14 @@
     rid(("OB", 1))
     b_sems = keys[("OB", 0)]
 
-    def give_back():
+    def give_back(src, dst, sem, only):
         for j in range(2):
             other = jnp.logical_not(loops & (j == x % 2))
-            for src, dst, sem, which in (
-                (FA, OA, rid(("OA",)), other & (core == j)),
-                (FB, OB.at[core], rsem.at[b_sems + core], other),
-            ):
-                i = sent[0]
-                sent[0] += 1
-                backs.append((which, pltpu.make_async_remote_copy(src, dst, ssem.at[i], sem, device_id=sources[j])))
-        for which, c in backs:
+            which = other & (core == j) if only else other
+            i = sent[0]
+            sent[0] += 1
+            c = pltpu.make_async_remote_copy(src, dst, ssem.at[i], sem, device_id=sources[j])
+            backs.append((which, c))
 
             @pl.when(which)
             def _():
@@ -470,8 +474,13 @@
 
         @pl.when(loops)
         def _():
-            OA[...] = FA[...]
-            OB[core] = FB[...]
+            dst[...] = src[...]
+
+    def give_a():
+        give_back(FA, OA, rid(("OA",)), True)
+
+    def give_b():
+        give_back(FB, OB.at[core], rsem.at[b_sems + core], False)
 
     def take_back():
         @pl.when(jnp.logical_not(loops))
@@ -496,18 +505,19 @@
             gin[...] = jnp.concatenate([b_rows[8:], a_rows], 0).astype(bf16)
 
     steps = [
-        (tick, 0), (weights, 5, 15), (gh_in.wait,),
-        (tick, 1), (tick, 2),
+        (tick, 0), (weights, 3, 6), (gh_in.wait,),
+        (tick, 1), (weights, 6, 11),
+        (tick, 2), (weights, 11, 15),
         (sib_wait, 0), (partial_pre, 0),
         (tick, 3), (pre_middle, 0), (sib_wait, 1), (partial_pre, 1),
         (tick, 4), (activate, 0), (sib_wait, 2), (partial_pre, 2),
         (tick, 5), (pre_middle, 1), (grad_middle, 0),
-        (sib_wait, 3), (partial_pre, 3), (sib_wait, 4), (partial_pre, 4),
-        (pre_middle, 2), (input_terms, 0), (activate, 2), (pre_middle, 3), (activate, 4), (grad_middle, 2),
-        (ay_begin, 0), (activate, 3), (activate, 1), (hidden_out,),
-        (input_terms, 4), (grad_middle, 3), (ay_middle, 0),
-        (input_terms, 2), (grad_middle, 1),
-        (ay_begin, 7), (ay_begin, 3), (ay_begin, 4),
+        (sib_wait, 3), (partial_pre, 3), (pre_middle, 2), (sib_wait, 4), (partial_pre, 4),
+        (transposes, 0, 15), (pre_middle, 3), (activate, 2), (activate, 4),
+        (input_terms, 0), (activate, 3), (activate, 1), (hidden_out,),
+        (grad_middle, 2), (ay_begin, 0),
+        (input_terms, 4), (ay_middle, 0), (grad_middle, 3),
+        (input_terms, 2), (ay_begin, 7), (ay_begin, 3), (ay_begin, 4), (grad_middle, 1),
         (input_terms, 3),
         (ay_end, 0), (cb_wait, 7, 6, 5),
         (b_step, 0, yf2, yf1, yb1, y),
@@ -517,22 +527,20 @@
         (b_step, 1, yf2, yf1, yb1, y),
         (ay_end, 6), (a_step, 0), (ay_end, 5),
         (cb_wait, 2, 1, 0), (ay_begin, 2), (ay_begin, 1), (ay_end, 4), (ay_end, 3),
-        (weight_far, 0, 3),
         (b_step, 2, yf2, yf1, yb1, y),
         (a_step, 1),
-        (weight_far, 3, 6),
+        (weight_far, 0, 3),
         (ay_middle, 2), (ay_middle, 1),
         (b_step, 3, yf2, yf1, yb1, y),
+        (weight_far, 3, 5),
         (ay_end, 2), (a_step, 2), (ay_end, 1),
-        (weight_far, 6, 10),
         (b_step, 4, yf2, yf1, yb1, y),
-        (weight_far, 10, 12),
+        (weight_far, 5, 9),
         (a_step, 3),
-        (weight_far, 12, 15), (weight_grad, 0, 5),
-        (b_end,),
-        (a_step, 4),
-        (give_back,),
-        (weight_grad, 5, 15),
+        (weight_far, 9, 15),
+        (b_end,), (give_b,),
+        (a_step, 4), (give_a,),
+        (weight_grad, 0, 15),
         (take_back,),
     ]
     for step, *args in steps:
@@ -540,7 +548,8 @@
 
     @pl.when(jnp.logical_not(loops))
     def _():
-        swap.wait_send()
+        for c in swaps:
+            c.wait_send()
 
     for which, c in backs:
 
@@ -586,7 +595,7 @@
         scratch_shapes=[
             vm(24, D4), pltpu.SMEM((H // 128, D4 // 128), f32),
             vm(D4, H), vm(D4, H), vm(H, D4),
-            vm(ROWS, BW), vm(2, ROWS, BW),
+            vm(U, D4), y_buf, vm(2, U, BW),
             vm(NY, NZ, ROWS, D4),
             vm(NZ, ROWS, H), vm(NZ, ROWS, H),
             vm(NY, NZ, ROWS, H), vm(NX - 1, NZ, ROWS, H), vm(NZ, ROWS, H), vm(NY, NZ, ROWS, H),

time: 103 us -> 100 us (0.971)
  Pallas kernels: 102 us -> 99.7 us
    pallas_call x1, Pallas kernels: 100 us -> 98.2 us  [shards(): pl.pallas_call(kernel, out_shape=out_shape, in_specs=[far, far, far, far]...]
where the time goes in v5:
time: 100 us
  Pallas kernels  99.7 us (100%)
    pallas_call x1, Pallas kernels, shards(): pl.pallas_call(kernel, out_shape=out_shape, in_specs=[far, far, far, far]...  98.2 us

profile of v5, /device:TPU:17, one launch (start us, length us, event | category | flops | bytes accessed | tf_op | source)
XLA Modules:
  0.0 100.3 jit_solution(2490754088362472124)
XLA Ops:
  0.6 98.2 %grid_layer.1 = (bf16[8,48,512]{2,1,0:T(8,128)(2,1)S(1)}, bf16[24,1920]{1,0:T(8,128)(2,1)S(1)}, bf16[1920,512]{1,0:T(8,128)(2,1)S(1)}) custom-call(bf16[24,1920]{1,0:T(8,128)(2,1)} %bitcast.6, bf16[1920,512]{1,0:T(8,128)(2,1)} %lev.1, f32[4,15]{1,0:T(4,128)} %bitcast.7, bf16[8,48,512]{2,1,0:T(8,128)(2,1)} %bitcast.5), custom_call_target="tpu_custom_call" | custom-call | tf_op jit(solution)/shard_map/grid_layer/pallas_call | solution.py:590
  98.8 1.5 %flush.1 = (bf16[8,48,512]{2,1,0:T(8,128)(2,1)}, bf16[24,1920]{1,0:T(8,128)(2,1)}, bf16[1920,512]{1,0:T(8,128)(2,1)}) custom-call(bf16[8,48,512]{2,1,0:T(8,128)(2,1)S(1)} %get-tuple-element.9.h, bf16[24,1920]{1,0:T(8,128)(2,1)S(1)} %get-tuple-element.10.i, bf16[1920,512]{1,0:T(8,128)(2,1)S(1)} %get-tuple-element.11.w), custom_call_target="tpu_custom_call" | custom-call | tf_op jit(solution)/shard_map/flush/pallas_call | solution.py:618

commit v6 on v5

--- a/solution.py
+++ b/solution.py
@@ -540,7 +540,7 @@
         (weight_far, 9, 15),
         (b_end,), (give_b,),
         (a_step, 4), (give_a,),
-        (weight_grad, 0, 15),
+        (weight_grad, 0, 5), (weight_grad, 5, 9), (weight_grad, 9, 12), (weight_grad, 12, 15),
         (take_back,),
     ]
     for step, *args in steps:

time: 100 us -> 100 us (level)
  no operation moved by 1% of the time
where the time goes in v6:
time: 100 us
  Pallas kernels  99.7 us (100%)
    pallas_call x1, Pallas kernels, shards(): pl.pallas_call(kernel, out_shape=out_shape, in_specs=[far, far, far, far]...  98.2 us

profile of v6, /device:TPU:17, one launch (start us, length us, event | category | flops | bytes accessed | tf_op | source)
XLA Modules:
  0.0 100.3 jit_solution(7331873131809257025)
XLA Ops:
  0.6 98.2 %grid_layer.1 = (bf16[8,48,512]{2,1,0:T(8,128)(2,1)S(1)}, bf16[24,1920]{1,0:T(8,128)(2,1)S(1)}, bf16[1920,512]{1,0:T(8,128)(2,1)S(1)}) custom-call(bf16[24,1920]{1,0:T(8,128)(2,1)} %bitcast.6, bf16[1920,512]{1,0:T(8,128)(2,1)} %lev.1, f32[4,15]{1,0:T(4,128)} %bitcast.7, bf16[8,48,512]{2,1,0:T(8,128)(2,1)} %bitcast.5), custom_call_target="tpu_custom_call" | custom-call | tf_op jit(solution)/shard_map/grid_layer/pallas_call | solution.py:590
  98.8 1.5 %flush.1 = (bf16[8,48,512]{2,1,0:T(8,128)(2,1)}, bf16[24,1920]{1,0:T(8,128)(2,1)}, bf16[1920,512]{1,0:T(8,128)(2,1)}) custom-call(bf16[8,48,512]{2,1,0:T(8,128)(2,1)S(1)} %get-tuple-element.9.h, bf16[24,1920]{1,0:T(8,128)(2,1)S(1)} %get-tuple-element.10.i, bf16[1920,512]{1,0:T(8,128)(2,1)S(1)} %get-tuple-element.11.w), custom_call_target="tpu_custom_call" | custom-call | tf_op jit(solution)/shard_map/flush/pallas_call | solution.py:618
